TPU v7x, 256 devices: a whole 4x4x8 slice. The times are simulated.
256 devices in a mesh: frame: 8 (over y, z_lo), head: 16 (over x, z_hi), tok: 2 (over core).
Axes of the slice: x: 4, y: 4, z: 8 (z_hi: 4, z_lo: 2; z = z_hi * 2 + z_lo), core: 2. Of those that a mesh axis runs over, the one named last changes fastest.
Arguments:
- queue: bfloat16 [16, 1024, 3072], P('frame', ('head', 'tok')), may hold values from -6 to 6
- timesteps: int32 [16], P('frame'), may hold values from 0 to 49
- mod_table: float32 [50, 3, 3072], replicated, may hold values from -3 to 3
- w_qkv: bfloat16 [3072, 16, 384], P(None, 'head'), may hold values from -0.108253175 to 0.108253175
- norm_gains: float32 [2, 128], replicated, may hold values from 0.7 to 4
- w_out: bfloat16 [16, 128, 3072], P('head'), may hold values from -0.125 to 0.125
- noise_frame: bfloat16 [1024, 3072], P(('head', 'tok')), may hold values from -6 to 6
Outputs:
- queue_next: bfloat16 [16, 1024, 3072], P('frame', ('head', 'tok'))
All inputs are finite; a program needn't handle non-finite values.
Results may differ from a plain program's by a relative error of at most 0.012.
Values may be sent and summed in bfloat16 or wider, within the bound.
A program may use at most 64 MiB of HBM per device.

v0:
```python
import jax
import jax.numpy as jnp
from jax import lax
from jax.sharding import PartitionSpec as P


def padded(cells, sides, width):
    for axis, dim in sides:
        count = lax.axis_size(axis)
        ends = count - 1
        head = lax.slice_in_dim(cells, 0, width, axis=dim)
        tail = lax.slice_in_dim(cells, cells.shape[dim] - width, cells.shape[dim], axis=dim)
        cells = jnp.concatenate(
            [
                lax.ppermute(tail, axis, [(i, (i + 1) % count) for i in range(ends)]),
                cells,
                lax.ppermute(head, axis, [((i + 1) % count, i) for i in range(ends)]),
            ],
            axis=dim,
        )
    return cells


def from_behind(value, axis, steps):
    count = lax.axis_size(axis)
    first, last = (max(0, -steps), min(count, count - steps))
    return lax.ppermute(value, axis, [(source, source + steps) for source in range(first, last)])


def rms_scale(values, gain):
    return values * lax.rsqrt(jnp.mean(values * values, axis=-1, keepdims=True) + 1e-06) * gain


def attend_rows(queries, key_rows, val_rows, valid, inv_scale):
    scores = (
        lax.dot_general(
            queries, key_rows, (((1,), (1,)), ((), ())), preferred_element_type=jnp.float32
        )
        * inv_scale
    )
    scores = jnp.where(valid[None, :], scores, -1e30)
    peak = jnp.max(scores, axis=-1, keepdims=True)
    probs = jnp.exp(scores - peak)
    total_p = jnp.sum(probs, axis=-1, keepdims=True)
    mixed = jnp.dot(probs.astype(jnp.bfloat16), val_rows, preferred_element_type=jnp.float32)
    return (mixed / total_p).astype(jnp.bfloat16)


def body(queue, timesteps, mod_table, w_qkv, norm_gains, w_out, noise_frame):
    slots = queue.shape[0]
    head_size = w_out.shape[1]
    level_count = mod_table.shape[0]
    onehot = (timesteps[:, None] == jnp.arange(level_count, dtype=jnp.int32)[None, :]).astype(
        jnp.float32
    )
    mods = jnp.einsum("fs,scd->fcd", onehot, mod_table, precision=lax.Precision.HIGHEST)
    shift_v, scale_v, gate_v = (mods[:, 0], mods[:, 1], mods[:, 2])
    xfull = queue.astype(jnp.float32)
    mean = jnp.mean(xfull, axis=-1, keepdims=True)
    centred = xfull - mean
    normed = centred * lax.rsqrt(jnp.mean(centred * centred, axis=-1, keepdims=True) + 1e-06)
    modulated = (normed * (1.0 + scale_v[:, None, :]) + shift_v[:, None, :]).astype(jnp.bfloat16)
    weight = w_qkv[:, 0, :]
    qkv = jnp.einsum(
        "fsd,dc->fsc",
        lax.all_gather(modulated, "head", axis=1, tiled=True),
        weight,
        preferred_element_type=jnp.float32,
    )
    query = rms_scale(qkv[..., :head_size], norm_gains[0])
    keys = rms_scale(qkv[..., head_size : 2 * head_size], norm_gains[1])
    qkv_rows = jnp.concatenate([query, keys, qkv[..., 2 * head_size :]], axis=-1).astype(
        jnp.bfloat16
    )
    query = qkv_rows[..., :head_size]
    kv_local = qkv_rows[..., head_size:]
    kv_frame = lax.all_gather(kv_local, "tok", axis=1, tiled=True)
    kv_ext = padded(kv_frame, (("frame", 0),), 1)
    frame_tokens = kv_frame.shape[1]
    total_frames = slots * lax.axis_size("frame")
    first_slot = lax.axis_index("frame") * slots
    inv_scale = 1.0 / jnp.sqrt(jnp.float32(head_size))
    q_rows = query.shape[1]
    outputs = []
    for slot in range(slots):
        window = kv_ext[slot : slot + 3].reshape(3 * frame_tokens, 2 * head_size)
        key_rows = window[:, :head_size]
        val_rows = window[:, head_size:]
        global_frame = first_slot + slot - 1 + jnp.arange(3, dtype=jnp.int32)
        valid = jnp.repeat((global_frame >= 0) & (global_frame < total_frames), frame_tokens)
        blocks = query[slot].reshape(q_rows // q_rows, q_rows, head_size)
        mixed = lax.map(
            lambda rows: attend_rows(rows, key_rows, val_rows, valid, inv_scale), blocks
        )
        outputs.append(mixed.reshape(q_rows, head_size))
    attn = jnp.stack(outputs, axis=0)
    shards = lax.axis_size("head")
    per_shard = q_rows // shards
    attn_split = jnp.transpose(attn.reshape(slots, shards, per_shard, head_size), (1, 0, 2, 3))
    out_weight = w_out[0]
    rows = attn_split
    contrib = jnp.einsum("hfsc,cd->hfsd", rows, out_weight, preferred_element_type=jnp.float32)
    proj = lax.psum_scatter(
        lax.optimization_barrier(contrib.astype(jnp.bfloat16))
        .astype(jnp.float32)
        .astype(jnp.bfloat16),
        "head",
        scatter_dimension=0,
        tiled=True,
    ).astype(jnp.float32)[0]
    block_out = (xfull + gate_v[:, None, :] * proj).astype(jnp.bfloat16)
    arrived = from_behind(block_out[slots - 1 :], "frame", 1)
    entering = jnp.where(lax.axis_index("frame") == 0, noise_frame[None], arrived)
    return jnp.concatenate([entering, block_out[: slots - 1]], axis=0)


def solution(mesh):
    return jax.shard_map(
        body,
        mesh=mesh,
        in_specs=(
            P("frame", ("head", "tok"), None),
            P("frame"),
            P(),
            P(None, "head", None),
            P(),
            P("head", None, None),
            P(("head", "tok"), None),
        ),
        out_specs=P("frame", ("head", "tok"), None),
        check_vma=False,
    )
```

profile of v0, /device:TPU:1, one launch (start us, length us, event | category | flops | bytes accessed | tf_op | source)
XLA Modules:
  0.0 311.2 jit_solution(15830352089770906445)
XLA Ops:
  6.5 0.0 copy-start
  6.5 0.0 all-gather.3.cloned.1.call-start
  6.5 2.5 fusion.43
  9.1 1.1 convert_reduce_fusion
  10.2 1.3 fusion.28
  11.5 2.0 fusion.31
  13.4 0.0 all-gather.3.cloned.1.call-update
  13.5 0.0 all-gather.5.cloned.1.call-start
  13.5 0.8 slice_bitcast_fusion.7
  14.3 93.9 %all-gather.3.cloned.1.call-done = bf16[2,512,3072]{2,1,0:T(8,128)(2,1)} async-done(((bf16[2,32,3072]{2,1,0:T(8,128)(2,1)}), bf16[2,512,3072]{2,1,0:T(8,128)(2,1)}) %all-gather.3.cloned.1.call-update) | async-done | bytes 6291472 | tf_op jit(solution)/shard_map/all_gather | solution.py:66
  108.2 0.0 copy-done
  108.2 4.8 %fusion.12 = f32[2,512,384]{1,2,0:T(8,128)S(1)} fusion(bf16[2,512,3072]{2,1,0:T(8,128)(2,1)} %all-gather.3.cloned.1.call-done, bf16[3072,1,384]{2,0,1:T(8,128)(2,1)S(1)} %copy-done), kind=kOutput, calls=%fused_computation.15 | convolution fusion | flops 2415919104 | bytes 10223616 | tf_op jit(solution)/shard_map/fsd,dc->fsc/dot_general | solution.py:64
  113.0 0.1 multiply_reduce_fusion.1
  113.2 0.1 multiply_convert_fusion.1
  113.4 0.8 pad_maximum_fusion.2
  114.2 0.0 all-gather.5.cloned.1.call-update
  114.2 0.0 reduce-scatter.2.cloned.1.call-start
  114.2 20.0 %all-gather.5.cloned.1.call-done = bf16[2,1024,256]{1,2,0:T(8,128)(2,1)} async-done(((bf16[2,512,256]{1,2,0:T(8,128)(2,1)}), bf16[2,1024,256]{1,2,0:T(8,128)(2,1)}) %all-gather.5.cloned.1.call-update) | async-done | bytes 1048592 | tf_op jit(solution)/shard_map/all_gather | solution.py:77
  134.3 2.2 fusion.53
  136.5 2.9 collective-permute-start
  139.5 1.5 collective-permute-start.1
  141.0 0.1 broadcast_in_dim.59
  141.1 0.1 broadcast_in_dim.63
  141.2 9.7 %collective-permute-done = bf16[1,1024,256]{1,2,0:T(8,128)(2,1)S(1)} collective-permute-done((bf16[1,1024,256]{1,2,0:T(8,128)(2,1)}, bf16[1,1024,256]{1,2,0:T(8,128)(2,1)S(1)}, u32[]{:S(2)}, u32[]{:S(2)}) %collective-permute-start) | collective-permute-done | bytes 524320 | tf_op jit(solution)/shard_map/ppermute | solution.py:15
  150.8 13.1 %collective-permute-done.1 = bf16[1,1024,256]{1,2,0:T(8,128)(2,1)} collective-permute-done((bf16[1,1024,256]{1,2,0:T(8,128)(2,1)}, bf16[1,1024,256]{1,2,0:T(8,128)(2,1)}, u32[]{:S(2)}, u32[]{:S(2)}) %collective-permute-start.1) | collective-permute-done | bytes 524320 | tf_op jit(solution)/shard_map/ppermute | solution.py:17
  163.9 3.6 %pad_maximum_fusion = (bf16[3,1024,256]{1,2,0:T(8,128)(2,1)}, bf16[3,1024,256]{1,2,0:T(8,128)(2,1)}) fusion(bf16[2,1024,256]{1,2,0:T(8,128)(2,1)} %all-gather.5.cloned.1.call-done, bf16[1,1024,256]{1,2,0:T(8,128)(2,1)S(1)} %collective-permute-done, bf16[1,1024,256]{1,2,0:T(8,128)(2,1)} %collective-permute-done.1), kind=kLoop, calls=%fused_computation.17 | loop fusion | flops 1572864 | bytes 5242880 | tf_op jit(solution)/shard_map/concatenate | solution.py:13
  167.5 2.6 copy.12
  170.1 0.0 copy-start.2
  170.1 2.5 fusion
  172.6 1.4 fusion.2
  174.0 0.0 copy-done.2
  174.0 1.4 fusion.17
  175.4 2.6 copy.13
  178.0 0.0 copy-start.3
  178.0 2.5 fusion.1
  180.5 1.4 fusion.4
  181.9 0.0 copy-done.3
  181.9 0.0 copy-start.4
  181.9 1.4 fusion.23
  183.3 0.0 copy-done.4
  183.3 0.0 copy-start.1
  183.3 0.0 copy-start.5
  183.4 4.4 %convolution_convert_fusion = bf16[16,2,32,3072]{3,2,1,0:T(8,128)(2,1)} fusion(bf16[1,128,3072]{2,1,0:T(8,128)(2,1)S(1)} %copy-done.4, bf16[1,16,32,128]{3,2,0,1:T(8,128)(2,1)S(1)} %bitcast.58, bf16[1,16,32,128]{3,2,0,1:T(8,128)(2,1)S(1)} %bitcast.57), kind=kOutput, calls=%fused_computation.4 | convolution fusion | flops 808583168 | bytes 7340032 | tf_op jit(solution)/shard_map/hfsc,cd->hfsd/dot_general | solution.py:102
  187.8 0.0 reduce-scatter.2.cloned.1.call-update
  187.8 108.6 %reduce-scatter.2.cloned.1.call-done = bf16[1,2,32,3072]{3,2,1,0:T(8,128)(2,1)} async-done(((bf16[16,2,32,3072]{3,2,1,0:T(8,128)(2,1)}), bf16[1,2,32,3072]{3,2,1,0:T(8,128)(2,1)}) %reduce-scatter.2.cloned.1.call-update) | async-done | bytes 393232 | tf_op jit(solution)/shard_map/reduce_scatter | solution.py:103
  296.5 0.0 copy-done.1
  296.5 1.1 fusion.32
  297.6 3.2 %collective-permute-start.2 = (bf16[1,32,3072]{2,1,0:T(8,128)(2,1)S(1)}, bf16[1,32,3072]{2,1,0:T(8,128)(2,1)S(1)}, u32[]{:S(2)}, u32[]{:S(2)}) collective-permute-start(bf16[1,32,3072]{2,1,0:T(8,128)(2,1)S(1)} %get-tuple-element.41), channel_id=1, source_target_pairs={{0,32},{32,64},{64,96},{96,128},{128,160},{160,192},{192,224},{1,3... | collective-permute-start | bytes 589832 | tf_op jit(solution)/shard_map/ppermute | solution.py:27
  300.8 3.0 collective-permute-done.2
  303.9 0.0 copy-done.5
  303.9 0.8 pad_maximum_fusion.3
  (11 shorter events, 0.2 us)
Async XLA Ops:
  6.5 101.7 %copy-start = (bf16[3072,1,384]{2,0,1:T(8,128)(2,1)S(1)}, bf16[3072,1,384]{2,0,1:T(8,128)(2,1)}, u32[]{:S(2)}) copy-start(bf16[3072,1,384]{2,0,1:T(8,128)(2,1)} %param.10) | copy-start | bytes 7077892
  6.5 101.7 %all-gather.3.cloned.1.call-start = ((), (), s32[]{:S(2)}) async-start(), calls=%async_computation.1 | async-start | bytes 6684672 | tf_op jit(solution)/shard_map/all_gather | solution.py:66
  13.5 120.8 %all-gather.5.cloned.1.call-start = ((), (), s32[]{:S(2)}) async-start(), calls=%async_computation.2 | async-start | bytes 1572864 | tf_op jit(solution)/shard_map/all_gather | solution.py:77
  114.2 182.3 %reduce-scatter.2.cloned.1.call-start = ((), (), s32[]{:S(2)}) async-start(), calls=%async_computation.3 | async-start | bytes 6684672 | tf_op jit(solution)/shard_map/reduce_scatter | solution.py:103
  136.5 14.3 %collective-permute-start = (bf16[1,1024,256]{1,2,0:T(8,128)(2,1)}, bf16[1,1024,256]{1,2,0:T(8,128)(2,1)S(1)}, u32[]{:S(2)}, u32[]{:S(2)}) collective-permute-start(bf16[1,1024,256]{1,2,0:T(8,128)(2,1)} %get-tuple-element.39), channel_id=1, source_target_pairs={{0,32},{32,64},{64,96},{96,128},{128,160},{160,192},{192,224},{1,3... | collective-permute-start | bytes 1572872 | tf_op jit(solution)/shard_map/ppermute | solution.py:15
  139.5 24.5 %collective-permute-start.1 = (bf16[1,1024,256]{1,2,0:T(8,128)(2,1)}, bf16[1,1024,256]{1,2,0:T(8,128)(2,1)}, u32[]{:S(2)}, u32[]{:S(2)}) collective-permute-start(bf16[1,1024,256]{1,2,0:T(8,128)(2,1)} %get-tuple-element.40), channel_id=1, source_target_pairs={{32,0},{64,32},{96,64},{128,96},{160,128},{192,160},{224,192},{33,... | collective-permute-start | bytes 1572872 | tf_op jit(solution)/shard_map/ppermute | solution.py:17
  170.1 3.9 %copy-start.2 = (bf16[3,1024,256]{2,1,0:T(8,128)(2,1)S(1)}, bf16[3,1024,256]{2,1,0:T(8,128)(2,1)}, u32[]{:S(2)}) copy-start(bf16[3,1024,256]{2,1,0:T(8,128)(2,1)} %copy.12) | copy-start | bytes 4718596
  178.0 3.9 %copy-start.3 = (bf16[3,1024,256]{2,1,0:T(8,128)(2,1)S(1)}, bf16[3,1024,256]{2,1,0:T(8,128)(2,1)}, u32[]{:S(2)}) copy-start(bf16[3,1024,256]{2,1,0:T(8,128)(2,1)} %copy.13) | copy-start | bytes 4718596
  181.9 1.4 copy-start.4
  183.3 113.1 %copy-start.1 = (bf16[2,32,3072]{2,1,0:T(8,128)(2,1)S(1)}, bf16[2,32,3072]{2,1,0:T(8,128)(2,1)}, u32[]{:S(2)}) copy-start(bf16[2,32,3072]{2,1,0:T(8,128)(2,1)} %param.7) | copy-start | bytes 1179652
  183.3 120.5 %copy-start.5 = (bf16[32,3072]{1,0:T(8,128)(2,1)S(1)}, bf16[32,3072]{1,0:T(8,128)(2,1)}, u32[]{:S(2)}) copy-start(bf16[32,3072]{1,0:T(8,128)(2,1)} %param.13) | copy-start | bytes 589828
  297.6 6.3 %collective-permute-start.2 = (bf16[1,32,3072]{2,1,0:T(8,128)(2,1)S(1)}, bf16[1,32,3072]{2,1,0:T(8,128)(2,1)S(1)}, u32[]{:S(2)}, u32[]{:S(2)}) collective-permute-start(bf16[1,32,3072]{2,1,0:T(8,128)(2,1)S(1)} %get-tuple-element.41), channel_id=1, source_target_pairs={{0,32},{32,64},{64,96},{96,128},{128,160},{160,192},{192,224},{1,3... | collective-permute-start | bytes 589832 | tf_op jit(solution)/shard_map/ppermute | solution.py:27
Sparse Core Ops, SparseCore 0:
  13.6 94.5 all-gather.2
  114.3 19.9 all-gather.4
  187.9 108.4 reduce-scatter.1
where the time goes:
time: 315 us; the launch traced here: 311 us
  waiting for transfers between devices  248 us (79%)
  matrix products  19.4 us (6%)
  other arithmetic  13.8 us (4%)
  between operations  13.3 us (4%)
  local copies, waits for them, and re-layouts  8.51 us (3%)
  starting transfers between devices  7.71 us (2%)
    reduce_scatter x1, waiting for transfers between devices, body(): lax.psum_scatter(lax.optimization_barrier(contrib.astype(jnp.bfloat16)).a...  109 us
    all_gather x1, waiting for transfers between devices, body(): lax.all_gather(modulated, 'head', axis=1, tiled=True)  93.9 us
    all_gather x1, waiting for transfers between devices, body(): kv_frame = lax.all_gather(kv_local, 'tok', axis=1, tiled=True)  20 us
    ppermute x1, waiting for transfers between devices, padded(): lax.ppermute(head, axis, [((i + 1) % count, i) for i in range(ends)])  13.1 us
    ppermute x1, waiting for transfers between devices, padded(): lax.ppermute(tail, axis, [(i, (i + 1) % count) for i in range(ends)])  9.68 us
  transfers between devices with their start and end apart: 6, of which 6 were waited for; matrix products, arithmetic and copies ran while one was open for 0% of the time, Pallas kernels for 0%

commit v1 on v0

v1 whole, which is shorter than its diff:
```python
import functools

import jax
import jax.numpy as jnp
from jax import lax
from jax.experimental import pallas as pl
from jax.experimental.pallas import tpu as pltpu
from jax.sharding import PartitionSpec as P

MESH = pl.DeviceIdType.MESH
NX = 4
NY = 4
NZ = 4
OWN, LEFT, RIGHT, OPP = 0, 1, 2, 3


class Place:
    def __init__(self):
        self.frame = lax.axis_index("frame")
        self.head = lax.axis_index("head")
        self.core = lax.axis_index("tok")
        self.x, self.zh = self.head // NZ, self.head % NZ
        self.y, self.zl = self.frame // 2, self.frame % 2

    def to(self, x=0, z=0, y=0, frame=0, flip=False, core=None):
        head = ((self.x + x) % NX) * NZ + (self.zh + z) % NZ
        own = ((self.y + y) % NY) * 2 + self.zl if frame == 0 else self.frame + frame
        tok = self.core if core is None else core
        tok = 1 - tok if flip else tok
        return (own, head, tok)


class Copies:
    def __init__(self, send, recv):
        self.send, self.recv, self.count, self.all = send, recv, 0, {}

    def make(self, name, src, dst, device):
        k = self.count
        self.count += 1
        copy = pltpu.make_async_remote_copy(
            src_ref=src,
            dst_ref=dst,
            send_sem=self.send.at[k],
            recv_sem=self.recv.at[k],
            device_id=device,
            device_id_type=MESH,
        )
        self.all[name] = copy
        return copy

    def start(self, name, src, dst, device):
        self.make(name, src, dst, device).start()

    def got(self, *names):
        for name in names:
            self.all[name].wait_recv()

    def sent(self, skip=()):
        for name, copy in self.all.items():
            if name not in skip:
                copy.wait_send()


def greet(devices, count):
    barrier = pltpu.get_barrier_semaphore()
    for device in devices:
        pl.semaphore_signal(barrier, inc=1, device_id=device, device_id_type=MESH)
    pl.semaphore_wait(barrier, count)


class Gather:
    def __init__(self, tag, copies, me, ring, source, held, half):
        self.tag, self.copies, self.me, self.ring = tag, copies, me, ring
        self.source, self.held, self.half = source, held, half
        self.mine = me.core * NY + me.y
        self.left = me.core * NY + (me.y + NY - 1) % NY
        self.right = me.core * NY + (me.y + 1) % NY
        self.far = me.core * NY + (me.y + 2) % NY

    def part(self, rel, eighth, which):
        return self.half(self.held, rel, eighth, which)

    def go(self, name, src, dst, device):
        self.copies.start(self.tag + name, src, dst, device)

    def got(self, *names):
        self.copies.got(*[self.tag + name for name in names])

    def ring_start(self):
        e = self.mine
        self.go("r", self.source.at[e], self.held.at[LEFT, e], self.me.to(**{self.ring: 1}))
        self.go("l", self.source.at[e], self.held.at[RIGHT, e], self.me.to(**{self.ring: -1}))

    def ring_relay(self):
        e = self.mine
        self.got("r")
        self.go("rr", self.part(LEFT, e, 0), self.part(OPP, e, 0), self.me.to(**{self.ring: 1}))
        self.y_start(LEFT)
        self.got("l")
        self.go("ll", self.part(RIGHT, e, 1), self.part(OPP, e, 1), self.me.to(**{self.ring: -1}))
        self.y_start(RIGHT)

    def ring_end(self):
        self.got("rr", "ll")
        self.y_start(OPP)

    def y_start(self, rel):
        n, e = str(rel), self.mine
        self.go("yr" + n, self.held.at[rel, e], self.held.at[rel, e], self.me.to(y=1))
        self.go("yl" + n, self.held.at[rel, e], self.held.at[rel, e], self.me.to(y=-1))
        self.go("s0" + n, self.held.at[rel, e], self.held.at[rel, e], self.me.to(flip=True))

    def y_relay(self, rel):
        n = str(rel)
        self.got("yr" + n)
        e = self.left
        self.go("yrr" + n, self.part(rel, e, 0), self.part(rel, e, 0), self.me.to(y=1))
        self.go("s1" + n, self.held.at[rel, e], self.held.at[rel, e], self.me.to(flip=True))
        self.got("yl" + n)
        e = self.right
        self.go("yll" + n, self.part(rel, e, 1), self.part(rel, e, 1), self.me.to(y=-1))
        self.go("s2" + n, self.held.at[rel, e], self.held.at[rel, e], self.me.to(flip=True))

    def y_end(self, rel):
        n = str(rel)
        self.got("yrr" + n, "yll" + n)
        e = self.far
        self.go("s3" + n, self.held.at[rel, e], self.held.at[rel, e], self.me.to(flip=True))

    def done(self, rel):
        n = str(rel)
        self.got("s0" + n, "s1" + n, "s2" + n, "s3" + n)


def rms_scale(values, gain):
    return values * lax.rsqrt(jnp.mean(values * values, axis=-1, keepdims=True) + 1e-06) * gain


def qkv_kernel(
    steps_ref, mod_hbm, queue_ref, w_hbm, gains_ref, q_out, kv_out,
    mod, xg, wg, sb, rb, local, send, recv,
):
    me = Place()
    core = me.core
    rows = queue_ref.shape[1]
    width = queue_ref.shape[2]
    hs = gains_ref.shape[1]
    partners = [me.to(flip=True)]
    for shift in (1, -1, 2):
        partners += [me.to(x=shift), me.to(x=shift, flip=True)]
    for shift in (1, -1):
        partners += [me.to(z=shift), me.to(y=shift)]
    mod_copy = pltpu.make_async_copy(mod_hbm, mod, local.at[0])
    mod_copy.start()
    own_copy = pltpu.make_async_copy(w_hbm, wg.at[OWN], local.at[1])
    own_copy.start()
    greet(partners, len(partners))

    copies = Copies(send, recv)
    seg = wg.shape[2] // 2
    weights = Gather(
        "w", copies, me, "x", w_hbm, wg,
        lambda ref, rel, e, which: ref.at[rel, e, pl.ds(which * seg, seg)],
    )
    weights.ring_start()

    mod_copy.wait()
    for slot in range(2):
        level = steps_ref[slot]
        x = queue_ref[slot].astype(jnp.float32)
        centred = x - jnp.mean(x, axis=-1, keepdims=True)
        normed = centred * lax.rsqrt(jnp.mean(centred * centred, axis=-1, keepdims=True) + 1e-06)
        mods = mod[level]
        xg[OWN, slot * rows : (slot + 1) * rows, :] = (
            normed * (1.0 + mods[1:2, :]) + mods[0:1, :]
        ).astype(jnp.bfloat16)
    copies.start("zr", xg.at[OWN], xg.at[LEFT], me.to(z=1))
    copies.start("zl", xg.at[OWN], xg.at[RIGHT], me.to(z=-1))

    weights.ring_relay()
    weights.ring_end()
    weights.y_relay(LEFT)
    copies.got("zr")
    copies.start("zrr", xg.at[LEFT, pl.ds(0, rows)], xg.at[OPP, pl.ds(0, rows)], me.to(z=1))
    copies.got("zl")
    copies.start("zll", xg.at[RIGHT, pl.ds(rows, rows)], xg.at[OPP, pl.ds(rows, rows)], me.to(z=-1))
    weights.y_relay(RIGHT)
    weights.y_end(LEFT)
    weights.y_relay(OPP)
    weights.y_end(RIGHT)
    copies.got("zrr", "zll")
    own_copy.wait()

    fold = jnp.float32(1.4426950408889634 / hs**0.5)
    tokens = NZ * rows

    def project(rel):
        xs = xg[...].reshape(NZ * 2 * rows, width)
        w = wg[rel].reshape(width, 3 * hs)
        qkv = jnp.dot(xs, w, preferred_element_type=jnp.float32)
        q = rms_scale(qkv[:, :hs], gains_ref[0:1, :] * fold)
        k = rms_scale(qkv[:, hs : 2 * hs], gains_ref[1:2, :])
        out = jnp.concatenate([q, k, qkv[:, 2 * hs :]], axis=-1).astype(jnp.bfloat16)
        out = out.reshape(NZ, 2, rows, 3 * hs)
        for slot in range(2):
            sb[rel, slot] = out[:, slot].reshape(tokens, 3 * hs)

    back = {LEFT: RIGHT, RIGHT: LEFT, OPP: OPP}
    shift = {LEFT: -1, RIGHT: 1, OPP: 2}
    project(OWN)
    copies.start("a0", sb.at[OWN, 1 - core], rb.at[OWN, core], me.to(flip=True))
    rb[OWN, core] = sb[OWN, core]
    for rel in (LEFT, RIGHT, OPP):
        if rel == OPP:
            weights.y_end(OPP)
        weights.done(rel)
        project(rel)
        n = str(rel)
        copies.start("a" + n, sb.at[rel, core], rb.at[back[rel], core], me.to(x=shift[rel]))
        copies.start(
            "b" + n, sb.at[rel, 1 - core], rb.at[back[rel], core], me.to(x=shift[rel], flip=True)
        )
    copies.got("a0")
    for rel in (LEFT, RIGHT, OPP):
        copies.got("a" + str(rel), "b" + str(rel))
    all_rows = rb[...].reshape(NX * 2 * tokens, 3 * hs)
    q_out[...] = all_rows[:, :hs]
    kv_out[...] = all_rows[:, hs:]
    copies.sent()


def out_kernel(
    steps_ref, mod_hbm, queue_ref, noise_ref, q_ref, kv_ref, w_hbm, out_ref,
    mod, kvb, kt, vx, oa, top, attn_s, attn_g, wo, po, pl_s, pr_s, rl, rr, fl, fr, qb, ob, ou,
    local, send, recv,
):
    me = Place()
    core, frame = me.core, me.frame
    frames = lax.axis_size("frame")
    hs = q_ref.shape[1]
    rows = queue_ref.shape[1]
    width = queue_ref.shape[2]
    keys = kv_ref.shape[0]
    half = width // 2
    chunk = keys // NX
    step = 2 * core - 1
    beside = frame + step
    has_beside = jnp.logical_and(beside >= 0, beside < frames)
    after = (frame + 1) % frames
    before = (frame + frames - 1) % frames

    mod_copy = pltpu.make_async_copy(mod_hbm, mod, local.at[0])
    mod_copy.start()
    own_copy = pltpu.make_async_copy(w_hbm, wo.at[OWN], local.at[1])
    own_copy.start()
    partners = [me.to(flip=True)]
    for shift in (1, -1):
        partners += [me.to(x=shift), me.to(z=shift), me.to(y=shift)]
    partners += [me.to(z=2)]
    partners += [(before, me.head, 1)]
    barrier = pltpu.get_barrier_semaphore()
    for device in partners:
        pl.semaphore_signal(barrier, inc=1, device_id=device, device_id_type=MESH)

    @pl.when(core == 1)
    def _():
        for tok in range(2):
            pl.semaphore_signal(
                barrier, inc=1, device_id=(after, me.head, tok), device_id_type=MESH
            )

    pl.semaphore_wait(barrier, len(partners) + 2 * core)

    copies = Copies(send, recv)
    side = copies.make("kv", kv_ref, kvb.at[1], (beside, me.head, 1 - core))
    copies.start("ks", kv_ref, kvb.at[0], me.to(flip=True))

    @pl.when(has_beside)
    def _():
        side.start()

    copies.start("qs", queue_ref.at[1 - core], qb.at[core], me.to(flip=True))
    weights = Gather(
        "w", copies, me, "z", w_hbm, wo,
        lambda ref, rel, e, which: ref.at[rel, e, :, pl.ds(which * half, half)],
    )
    weights.ring_start()

    def take(which, ref):
        kt[which] = ref[:, :hs].T
        vx[which, :, :hs] = ref[:, hs:]
        vx[which, :, hs:] = jnp.ones((keys, hs), jnp.bfloat16)

    take(0, kv_ref)
    weights.ring_relay()
    weights.ring_end()
    copies.got("ks")
    take(1, kvb.at[0])

    block = 128

    @pl.loop(0, keys // block)
    def _(i):
        at = pl.ds(pl.multiple_of(i * block, block), block)
        q = q_ref[at, :]
        scores = [jnp.dot(q, kt[j], preferred_element_type=jnp.float32) for j in range(2)]
        peak = jnp.maximum(
            jnp.max(scores[0], axis=-1, keepdims=True), jnp.max(scores[1], axis=-1, keepdims=True)
        )
        total = jnp.zeros((block, 2 * hs), jnp.float32)
        for j in range(2):
            p = jnp.exp2(scores[j] - peak).astype(jnp.bfloat16)
            total += jnp.dot(p, vx[j], preferred_element_type=jnp.float32)
        oa[at, :] = total
        top[at, :] = jnp.broadcast_to(peak, (block, hs))

    for rel in (LEFT, RIGHT, OPP):
        weights.y_relay(rel)

    @pl.when(has_beside)
    def _():
        side.wait_recv()
        take(2, kvb.at[1])

        @pl.loop(0, keys // block)
        def _(i):
            at = pl.ds(pl.multiple_of(i * block, block), block)
            q = q_ref[at, :]
            s = jnp.dot(q, kt[2], preferred_element_type=jnp.float32)
            old = top[at, :]
            peak = jnp.maximum(old[:, :1], jnp.max(s, axis=-1, keepdims=True))
            p = jnp.exp2(s - peak).astype(jnp.bfloat16)
            scale = jnp.exp2(old[:, :1] - peak)
            oa[at, :] = oa[at, :] * scale + jnp.dot(p, vx[2], preferred_element_type=jnp.float32)

    back = {LEFT: RIGHT, RIGHT: LEFT, OPP: OPP}
    shift = {LEFT: -1, RIGHT: 1, OPP: 2}
    for rx in (OPP, RIGHT, LEFT, OWN):
        o = oa[rx * chunk : (rx + 1) * chunk, :]
        attn = (o[:, :hs] / o[:, hs:]).astype(jnp.bfloat16).reshape(2, NZ, rows, hs)
        attn_g[rx, OWN] = attn[:, OWN].reshape(2 * rows, hs)
        for rz in (LEFT, RIGHT, OPP):
            attn_s[rx, rz] = attn[:, rz].reshape(2 * rows, hs)
            copies.start(
                f"a{rx}{rz}", attn_s.at[rx, rz], attn_g.at[rx, back[rz]], me.to(z=shift[rz])
            )
    for rel in (LEFT, RIGHT, OPP):
        weights.y_end(rel)
    for rel in (LEFT, RIGHT, OPP):
        weights.done(rel)
    own_copy.wait()

    def contribution(rx):
        copies.got(*[f"a{rx}{rz}" for rz in (LEFT, RIGHT, OPP)])
        a = jnp.concatenate([attn_g[rx, rz] for rz in range(NZ)], axis=-1)
        return jnp.dot(a, wo[...].reshape(NZ * hs, width), preferred_element_type=jnp.float32)

    po[...] = contribution(OPP).astype(jnp.bfloat16)
    copies.start("rl", po.at[:, pl.ds(0, half)], rl, me.to(x=1))
    copies.start("rr", po.at[:, pl.ds(half, half)], rr, me.to(x=-1))

    p = contribution(RIGHT)
    pr_s[1] = p[:, half:].astype(jnp.bfloat16)
    copies.start("fl1", pr_s.at[1], fl.at[1], me.to(x=1))
    copies.got("rl")
    pr_s[0] = (p[:, :half] + rl[...].astype(jnp.float32)).astype(jnp.bfloat16)
    copies.start("fl0", pr_s.at[0], fl.at[0], me.to(x=1))

    p = contribution(LEFT)
    pl_s[0] = p[:, :half].astype(jnp.bfloat16)
    copies.start("fr0", pl_s.at[0], fr.at[0], me.to(x=-1))
    copies.got("rr")
    pl_s[1] = (p[:, half:] + rr[...].astype(jnp.float32)).astype(jnp.bfloat16)
    copies.start("fr1", pl_s.at[1], fr.at[1], me.to(x=-1))

    p = contribution(OWN)
    mod_copy.wait()
    copies.got("qs")
    qb[core] = queue_ref[core]
    gate = mod[steps_ref[core]][2:3, :]
    copies.got("fl1", "fr0", "fl0", "fr1")
    for h in range(2):
        cols = slice(h * half, (h + 1) * half)
        proj = p[:, cols] + fl[h].astype(jnp.float32) + fr[h].astype(jnp.float32)
        for tok in range(2):
            ob[tok, :, cols] = (
                qb[tok, :, cols].astype(jnp.float32)
                + gate[:, cols] * proj[tok * rows : (tok + 1) * rows]
            ).astype(jnp.bfloat16)

    near = copies.make("o1", ob.at[1], ou.at[1], me.to(flip=True))
    next0 = copies.make("n0", ob.at[0], ou.at[0], (after, me.head, 0))
    k = copies.count
    next1 = pltpu.make_async_remote_copy(
        src_ref=ob.at[1], dst_ref=ou.at[0], send_sem=send.at[k], recv_sem=recv.at[k - 1],
        device_id=(after, me.head, 1), device_id_type=MESH,
    )

    @pl.when(core == 0)
    def _():
        near.start()
        out_ref[1] = ob[0]
        near.wait_send()

    sends_on = jnp.logical_and(core == 1, frame < frames - 1)

    @pl.when(sends_on)
    def _():
        next0.start()
        next1.start()

    @pl.when(core == 1)
    def _():
        near.wait_recv()
        out_ref[1] = ou[1]

    @pl.when(frame == 0)
    def _():
        out_ref[0] = noise_ref[...]

    @pl.when(frame > 0)
    def _():
        next0.wait_recv()
        out_ref[0] = ou[0]

    @pl.when(sends_on)
    def _():
        next0.wait_send()
        next1.wait_send()

    @pl.when(has_beside)
    def _():
        side.wait_send()

    copies.sent(skip=("kv", "o1", "n0"))


def body(queue, timesteps, mod_table, w_qkv, norm_gains, w_out, noise_frame):
    slots, rows, width = queue.shape
    hs = w_out.shape[1]
    bf16, f32 = jnp.bfloat16, jnp.float32
    vmem = pl.BlockSpec(memory_space=pltpu.VMEM)
    hbm = pl.BlockSpec(memory_space=pl.ANY)
    smem = pl.BlockSpec(memory_space=pltpu.SMEM)
    tokens = NZ * rows
    keys = NX * 2 * tokens
    eighth = width // 8
    limit = 56 * 1024 * 1024
    q, kv = pl.pallas_call(
        qkv_kernel,
        out_shape=(
            jax.ShapeDtypeStruct((keys, hs), bf16),
            jax.ShapeDtypeStruct((keys, 2 * hs), bf16),
        ),
        in_specs=[smem, hbm, vmem, hbm, vmem],
        out_specs=(vmem, vmem),
        scratch_shapes=[
            pltpu.VMEM(mod_table.shape, f32),
            pltpu.VMEM((NZ, 2 * rows, width), bf16),
            pltpu.VMEM((NX, 8, eighth, 3 * hs), bf16),
            pltpu.VMEM((NX, 2, tokens, 3 * hs), bf16),
            pltpu.VMEM((NX, 2, tokens, 3 * hs), bf16),
            pltpu.SemaphoreType.DMA((2,)),
            pltpu.SemaphoreType.DMA((48,)),
            pltpu.SemaphoreType.DMA((48,)),
        ],
        compiler_params=pltpu.CompilerParams(
            collective_id=0, has_side_effects=True, vmem_limit_bytes=limit
        ),
        name="qkv",
    )(timesteps, mod_table, queue, w_qkv.reshape(8, eighth, 3 * hs), norm_gains)
    half = width // 2
    return pl.pallas_call(
        out_kernel,
        out_shape=jax.ShapeDtypeStruct(queue.shape, bf16),
        in_specs=[smem, hbm, vmem, vmem, vmem, vmem, hbm],
        out_specs=vmem,
        scratch_shapes=[
            pltpu.VMEM(mod_table.shape, f32),
            pltpu.VMEM((2, keys, 2 * hs), bf16),
            pltpu.VMEM((3, hs, keys), bf16),
            pltpu.VMEM((3, keys, 2 * hs), bf16),
            pltpu.VMEM((keys, 2 * hs), f32),
            pltpu.VMEM((keys, hs), f32),
            pltpu.VMEM((NX, NZ, 2 * rows, hs), bf16),
            pltpu.VMEM((NX, NZ, 2 * rows, hs), bf16),
            pltpu.VMEM((NZ, 8, hs // 8, width), bf16),
            pltpu.VMEM((2 * rows, width), bf16),
            pltpu.VMEM((2, 2 * rows, half), bf16),
            pltpu.VMEM((2, 2 * rows, half), bf16),
            pltpu.VMEM((2 * rows, half), bf16),
            pltpu.VMEM((2 * rows, half), bf16),
            pltpu.VMEM((2, 2 * rows, half), bf16),
            pltpu.VMEM((2, 2 * rows, half), bf16),
            pltpu.VMEM((2, rows, width), bf16),
            pltpu.VMEM((2, rows, width), bf16),
            pltpu.VMEM((2, rows, width), bf16),
            pltpu.SemaphoreType.DMA((2,)),
            pltpu.SemaphoreType.DMA((64,)),
            pltpu.SemaphoreType.DMA((64,)),
        ],
        compiler_params=pltpu.CompilerParams(
            collective_id=1, has_side_effects=True, vmem_limit_bytes=limit
        ),
        name="attend",
    )(timesteps, mod_table, queue, noise_frame, q, kv, w_out.reshape(8, hs // 8, width))


def solution(mesh):
    return jax.shard_map(
        body,
        mesh=mesh,
        in_specs=(
            P("frame", ("head", "tok"), None),
            P("frame"),
            P(),
            P(None, "head", None),
            P(),
            P("head", None, None),
            P(("head", "tok"), None),
        ),
        out_specs=P("frame", ("head", "tok"), None),
        check_vma=False,
    )
```

time: 315 us -> 131 us (0.42); the launches traced: 311 us -> 131 us
  waiting for transfers between devices: 248 us -> 0 us
  Pallas kernels: 0 us -> 124 us
  matrix products: 19.4 us -> 0 us
  other arithmetic: 13.8 us -> 0 us
  between operations: 13.3 us -> 0.02 us
  starting transfers between devices: 7.71 us -> 0 us
    pallas_call x0 -> x2, Pallas kernels: none -> 124 us  [the longest x1 62.3 us: body(): pl.pallas_call(qkv_kernel, out_shape=(jax.ShapeDtypeStruct((keys, hs), bf...]
    all_gather x2 -> x0, waiting for transfers between devices: 114 us -> none  [the longest x1 93.9 us: body(): lax.all_gather(modulated, 'head', axis=1, tiled=True)]
    reduce_scatter x1 -> x0, waiting for transfers between devices: 109 us -> none  [body(): lax.psum_scatter(lax.optimization_barrier(contrib.astype(jnp.bfloat16)).a...]
    ppermute x3 -> x0, waiting for transfers between devices: 25.8 us -> none  [the longest x1 13.1 us: padded(): lax.ppermute(head, axis, [((i + 1) % count, i) for i in range(ends)])]
    dot_general x7 -> x0, matrix products: 19.4 us -> none  [the longest x2 4.91 us: attend_rows(): lax.dot_general(queries, key_rows, (((1,), (1,)), ((), ())), preferred_el...]
    ppermute x3 -> x0, starting transfers between devices: 7.62 us -> none  [the longest x1 3.21 us: from_behind(): lax.ppermute(value, axis, [(source, source + steps) for source in range(f...]
    unnamed x12 -> x2, local copies, waits for them, and re-layouts: 0.03 us -> 6.05 us
    reduce_sum x5 -> x0, other arithmetic: 5.37 us -> none  [the longest x2 2.85 us: attend_rows(): total_p = jnp.sum(probs, axis=-1, keepdims=True)]
  transfers between devices with their start and end apart: 6 -> 0, of which waited for: 6 -> 0; matrix products, arithmetic and copies ran while one was open for 0% -> 0% of each run, Pallas kernels for 0% -> 0%
where the time goes in v1:
time: 131 us
  Pallas kernels  124 us (95%)
  local copies, waits for them, and re-layouts  6.05 us (5%)
    pallas_call x1, Pallas kernels, body(): pl.pallas_call(qkv_kernel, out_shape=(jax.ShapeDtypeStruct((keys, hs), bf...  62.3 us
    pallas_call x1, Pallas kernels, body(): pl.pallas_call(out_kernel, out_shape=jax.ShapeDtypeStruct(queue.shape, bf...  62.2 us
    unnamed x2, local copies, waits for them, and re-layouts  6.05 us

profile of v1, /device:TPU:1, one launch (start us, length us, event | category | flops | bytes accessed | tf_op | source)
XLA Modules:
  0.0 130.6 jit_solution(7058898467397424920)
XLA Ops:
  0.0 4.3 %copy.9.mod_hbm = f32[50,3,3072]{2,1,0:T(4,128)} copy(f32[50,3,3072]{2,0,1:T(8,128)} %param.9) | data formatting | bytes 3686400 | tf_op args[2]
  4.3 62.3 %qkv.1 = (bf16[1024,128]{1,0:T(8,128)(2,1)}, bf16[1024,256]{1,0:T(8,128)(2,1)}) custom-call(s32[2]{0:T(128)} %steps_ref.3, f32[50,3,3072]{2,1,0:T(4,128)} %copy.9.mod_hbm, bf16[2,32,3072]{2,1,0:T(8,128)(2,1)} %queue_ref.3, bf16[8,384,384]{2,1,0:T(8,128)(2,1)} %bitcast.2, f32[2,128]{1,0:T(2,128)} %gains_ref.1), custom_call_target="tpu_custom_call" | custom-call | tf_op jit(solution)/shard_map/qkv/pallas_call | solution.py:449
  66.6 62.2 %attend.1 = bf16[2,32,3072]{2,1,0:T(8,128)(2,1)} custom-call(s32[2]{0:T(128)} %steps_ref.3, f32[50,3,3072]{2,1,0:T(4,128)} %copy.9.mod_hbm, bf16[2,32,3072]{2,1,0:T(8,128)(2,1)} %queue_ref.3, bf16[32,3072]{1,0:T(8,128)(2,1)} %noise_ref.1, bf16[1024,128]{1,0:T(8,128)(2,1)} %get-tuple-element.7.q_ref, bf16[1024,256]{1,0:T(8,128)(2,1)} %get-tuple-element.8.kv_ref, ...), custom_call_target="tpu_custom_call" | custom-call | tf_op jit(solution)/shard_map/attend/pallas_call | solution.py:473
  128.8 1.8 %copy.11 = bf16[2,32,3072]{2,1,0:T(8,128)(2,1)} copy(bf16[2,32,3072]{2,1,0:T(8,128)(2,1)} %attend.1) | data formatting | bytes 786432

commit v2 on v0

v2 whole, which is shorter than its diff:
```python
import functools

import jax
import jax.numpy as jnp
from jax import lax
from jax.experimental import pallas as pl
from jax.experimental.pallas import tpu as pltpu
from jax.sharding import PartitionSpec as P

MESH = pl.DeviceIdType.MESH
NX = 4
NY = 4
NZ = 4
OWN, LEFT, RIGHT, OPP = 0, 1, 2, 3


class Place:
    def __init__(self):
        self.frame = lax.axis_index("frame")
        self.head = lax.axis_index("head")
        self.core = lax.axis_index("tok")
        self.x, self.zh = self.head // NZ, self.head % NZ
        self.y, self.zl = self.frame // 2, self.frame % 2

    def to(self, x=0, z=0, y=0, frame=0, flip=False, core=None):
        head = ((self.x + x) % NX) * NZ + (self.zh + z) % NZ
        own = ((self.y + y) % NY) * 2 + self.zl if frame == 0 else self.frame + frame
        tok = self.core if core is None else core
        tok = 1 - tok if flip else tok
        return (own, head, tok)


class Copies:
    def __init__(self, send, recv):
        self.send, self.recv, self.count, self.all = send, recv, 0, {}

    def make(self, name, src, dst, device):
        k = self.count
        self.count += 1
        copy = pltpu.make_async_remote_copy(
            src_ref=src,
            dst_ref=dst,
            send_sem=self.send.at[k],
            recv_sem=self.recv.at[k],
            device_id=device,
            device_id_type=MESH,
        )
        self.all[name] = copy
        return copy

    def start(self, name, src, dst, device):
        self.make(name, src, dst, device).start()

    def got(self, *names):
        for name in names:
            self.all[name].wait_recv()

    def sent(self, skip=()):
        for name, copy in self.all.items():
            if name not in skip:
                copy.wait_send()


def greet(devices, count):
    barrier = pltpu.get_barrier_semaphore()
    for device in devices:
        pl.semaphore_signal(barrier, inc=1, device_id=device, device_id_type=MESH)
    pl.semaphore_wait(barrier, count)


class Gather:
    def __init__(self, tag, copies, me, ring, source, held, half, whole):
        self.tag, self.copies, self.me, self.ring = tag, copies, me, ring
        self.source, self.held, self.half, self.whole = source, held, half, whole
        self.mine = me.core * NY + me.y
        self.left = me.core * NY + (me.y + NY - 1) % NY
        self.right = me.core * NY + (me.y + 1) % NY
        self.far = me.core * NY + (me.y + 2) % NY

    def part(self, rel, eighth, which):
        return self.half(self.held, rel, eighth, which)

    def go(self, name, src, dst, device):
        self.copies.start(self.tag + name, src, dst, device)

    def got(self, *names):
        self.copies.got(*[self.tag + name for name in names])

    def ring_start(self):
        e = self.mine
        self.go("r", self.source(e), self.whole(self.held, LEFT, e), self.me.to(**{self.ring: 1}))
        self.go("l", self.source(e), self.whole(self.held, RIGHT, e), self.me.to(**{self.ring: -1}))

    def ring_relay(self):
        e = self.mine
        self.got("r")
        self.go("rr", self.part(LEFT, e, 0), self.part(OPP, e, 0), self.me.to(**{self.ring: 1}))
        self.y_start(LEFT)
        self.got("l")
        self.go("ll", self.part(RIGHT, e, 1), self.part(OPP, e, 1), self.me.to(**{self.ring: -1}))
        self.y_start(RIGHT)

    def ring_end(self):
        self.got("rr", "ll")
        self.y_start(OPP)

    def y_start(self, rel):
        n, e = str(rel), self.mine
        self.go("yr" + n, self.whole(self.held, rel, e), self.whole(self.held, rel, e), self.me.to(y=1))
        self.go("yl" + n, self.whole(self.held, rel, e), self.whole(self.held, rel, e), self.me.to(y=-1))
        self.go("s0" + n, self.whole(self.held, rel, e), self.whole(self.held, rel, e), self.me.to(flip=True))

    def y_relay(self, rel):
        n = str(rel)
        self.got("yr" + n)
        e = self.left
        self.go("yrr" + n, self.part(rel, e, 0), self.part(rel, e, 0), self.me.to(y=1))
        self.go("s1" + n, self.whole(self.held, rel, e), self.whole(self.held, rel, e), self.me.to(flip=True))
        self.got("yl" + n)
        e = self.right
        self.go("yll" + n, self.part(rel, e, 1), self.part(rel, e, 1), self.me.to(y=-1))
        self.go("s2" + n, self.whole(self.held, rel, e), self.whole(self.held, rel, e), self.me.to(flip=True))

    def y_end(self, rel):
        n = str(rel)
        self.got("yrr" + n, "yll" + n)
        e = self.far
        self.go("s3" + n, self.whole(self.held, rel, e), self.whole(self.held, rel, e), self.me.to(flip=True))

    def done(self, rel):
        n = str(rel)
        self.got("s0" + n, "s1" + n, "s2" + n, "s3" + n)


def rms_scale(values, gain):
    return values * lax.rsqrt(jnp.mean(values * values, axis=-1, keepdims=True) + 1e-06) * gain


def block_kernel(
    mods_ref, queue_ref, noise_ref, gains_ref, w_hbm, wo_hbm, out_ref,
    xg, wg, sb, rb, kvb, kt, vx, oa, top, attn_s, attn_g, wo, po, pr_s, pl_s, rl, rr, fl, fr,
    qb, ob, ou, local, send, recv,
):
    me = Place()
    core, frame = me.core, me.frame
    frames = lax.axis_size("frame")
    rows, width = queue_ref.shape[1:]
    hs = gains_ref.shape[1]
    bf16, f32 = jnp.bfloat16, jnp.float32
    half = width // 2
    tokens = NZ * rows
    keys = NX * 2 * tokens
    beside = frame + 2 * core - 1
    has_beside = jnp.logical_and(beside >= 0, beside < frames)
    after = (frame + 1) % frames
    before = (frame + frames - 1) % frames
    back = {LEFT: RIGHT, RIGHT: LEFT, OPP: OPP}
    shift = {LEFT: -1, RIGHT: 1, OPP: 2}

    own_w = pltpu.make_async_copy(w_hbm, wg.at[OWN], local.at[0])
    own_w.start()
    own_wo = pltpu.make_async_copy(wo_hbm, wo.at[OWN], local.at[1])
    own_wo.start()

    partners = [me.to(flip=True)]
    for step in (1, -1, 2):
        partners += [me.to(x=step), me.to(x=step, flip=True), me.to(z=step)]
    partners += [me.to(y=1), me.to(y=-1)]
    partners += [(before, me.head, 1)]
    barrier = pltpu.get_barrier_semaphore()
    for device in partners:
        pl.semaphore_signal(barrier, inc=1, device_id=device, device_id_type=MESH)

    @pl.when(core == 1)
    def _():
        for tok in range(2):
            pl.semaphore_signal(
                barrier, inc=1, device_id=(after, me.head, tok), device_id_type=MESH
            )

    pl.semaphore_wait(barrier, len(partners) + 2 * core)

    copies = Copies(send, recv)
    mine = me.core * NY + me.y
    seg = wg.shape[2]
    direct = seg // 4 // 32 * 32
    part = (seg - direct) // 2
    weights = Gather(
        "w", copies, me, "x", (lambda e: w_hbm.at[e, pl.ds(direct, 2 * part)]), wg,
        lambda ref, rel, e, which: ref.at[rel, e, pl.ds(direct + which * part, part)],
        lambda ref, rel, e: ref.at[rel, e, pl.ds(direct, 2 * part)],
    )
    weights.ring_start()
    quad = pl.ds(core * NY, NY)

    def rows_of(rel, first, count):
        return wg.at[rel, quad, pl.ds(first, count)]

    source = w_hbm.at[quad, pl.ds(0, direct)]
    copies.start("dr", source, rows_of(LEFT, 0, direct), me.to(x=1))
    copies.start("dl", source, rows_of(RIGHT, 0, direct), me.to(x=-1))

    for slot in range(2):
        x = queue_ref[slot].astype(f32)
        centred = x - jnp.mean(x, axis=-1, keepdims=True)
        normed = centred * lax.rsqrt(jnp.mean(centred * centred, axis=-1, keepdims=True) + 1e-06)
        xg[OWN, slot * rows : (slot + 1) * rows, :] = (
            normed * (1.0 + mods_ref[slot, 1:2, :]) + mods_ref[slot, 0:1, :]
        ).astype(bf16)
    first, second = pl.ds(0, rows), pl.ds(rows, rows)
    copies.start("zr0", xg.at[OWN, first], xg.at[LEFT, first], me.to(z=1))
    copies.start("zl1", xg.at[OWN, second], xg.at[RIGHT, second], me.to(z=-1))
    copies.start("zr1", xg.at[OWN, second], xg.at[LEFT, second], me.to(z=1))
    copies.start("zl0", xg.at[OWN, first], xg.at[RIGHT, first], me.to(z=-1))
    copies.start("qs", queue_ref.at[1 - core], qb.at[core], me.to(flip=True))

    weights.ring_relay()
    weights.ring_end()
    copies.got("zr0")
    copies.start("zrr", xg.at[LEFT, first], xg.at[OPP, first], me.to(z=1))
    copies.got("zl1")
    copies.start("zll", xg.at[RIGHT, second], xg.at[OPP, second], me.to(z=-1))
    copies.got("dr")
    low, high = direct // 2, direct - direct // 2
    copies.start("drr", rows_of(LEFT, 0, low), rows_of(OPP, 0, low), me.to(x=1))
    copies.start("ds1", rows_of(LEFT, 0, direct), rows_of(LEFT, 0, direct), me.to(flip=True))
    copies.got("dl")
    copies.start("dll", rows_of(RIGHT, low, high), rows_of(OPP, low, high), me.to(x=-1))
    copies.start("ds2", rows_of(RIGHT, 0, direct), rows_of(RIGHT, 0, direct), me.to(flip=True))
    weights.y_relay(LEFT)
    weights.y_relay(RIGHT)
    weights.y_end(LEFT)
    copies.got("drr", "dll")
    copies.start("ds3", rows_of(OPP, 0, direct), rows_of(OPP, 0, direct), me.to(flip=True))

    q_gain = gains_ref[0:1, :] * f32(1.4426950408889634 / hs**0.5)
    k_gain = gains_ref[1:2, :]
    groups = (pl.ds(0, NZ - 1), pl.ds(NZ - 1, 1))
    sizes = (NZ - 1, 1)

    def project(rel, group):
        which, count = groups[group], sizes[group]
        xs = xg[which].reshape(count * 2 * rows, width)
        w = wg[rel].reshape(width, 3 * hs)
        qkv = jnp.dot(xs, w, preferred_element_type=f32)
        q = rms_scale(qkv[:, :hs], q_gain)
        k = rms_scale(qkv[:, hs : 2 * hs], k_gain)
        out = jnp.concatenate([q, k, qkv[:, 2 * hs :]], axis=-1).astype(bf16)
        out = out.reshape(count, 2, rows, 3 * hs)
        for slot in range(2):
            sb[rel, slot, which] = out[:, slot]
        n = f"{rel}{group}"
        if rel == OWN:
            copies.start(
                "a" + n, sb.at[OWN, 1 - core, which], rb.at[core, which], me.to(flip=True)
            )
            rb[core, which] = sb[OWN, core, which]
            return
        spot = rb.at[back[rel] * 2 + core, which]
        copies.start("a" + n, sb.at[rel, core, which], spot, me.to(x=shift[rel]))
        copies.start("b" + n, sb.at[rel, 1 - core, which], spot, me.to(x=shift[rel], flip=True))

    def share(rel, group):
        n = f"{rel}{group}"
        copies.got("a" + n)
        if rel != OWN:
            copies.got("b" + n)
        spot = OWN if rel == OWN else back[rel]
        pair = pl.ds(spot * 2, 2)
        src = rb.at[pair, groups[group], :, pl.ds(hs, 2 * hs)]
        dst = kvb.at[1, pair, groups[group]]
        side = copies.make("kv" + n, src, dst, (beside, me.head, 1 - core))

        @pl.when(has_beside)
        def _():
            side.start()

        copies.start("ks" + n, src, kvb.at[0, pair, groups[group]], me.to(flip=True))

    own_w.wait()
    copies.got("zr1", "zl0")
    project(OWN, 0)
    weights.y_relay(OPP)
    weights.done(LEFT)
    copies.got("ds1")
    project(LEFT, 0)
    weights.y_end(RIGHT)
    weights.done(RIGHT)
    copies.got("ds2")
    project(RIGHT, 0)
    share(OWN, 0)
    copies.got("zrr", "zll")
    project(OWN, 1)
    project(LEFT, 1)
    project(RIGHT, 1)
    weights.y_end(OPP)
    weights.done(OPP)
    copies.got("ds3")
    project(OPP, 0)
    project(OPP, 1)
    outs = Gather(
        "o", copies, me, "z", (lambda e: wo_hbm.at[e]), wo,
        lambda ref, rel, e, which: ref.at[rel, e, :, pl.ds(which * half, half)],
        lambda ref, rel, e: ref.at[rel, e],
    )
    outs.ring_start()
    share(LEFT, 0)
    share(RIGHT, 0)
    share(OWN, 1)
    share(LEFT, 1)
    share(RIGHT, 1)
    share(OPP, 0)
    share(OPP, 1)
    names = [f"{rel}{group}" for rel in range(4) for group in range(2)]

    ones = jnp.ones((keys, hs), bf16)

    def take(which, kv):
        kt[which] = kv[:, :hs].T
        vx[which, :, :hs] = kv[:, hs:]
        vx[which, :, hs:] = ones

    take(0, rb[...].reshape(keys, 3 * hs)[:, hs:])
    outs.ring_relay()
    copies.got(*["ks" + n for n in names])
    take(1, kvb[0].reshape(keys, 2 * hs))
    outs.ring_end()

    block = tokens

    def queries(i):
        return rb[i].reshape(block, 3 * hs)[:, :hs]

    @pl.loop(0, 2 * NX)
    def _(i):
        q = queries(i)
        scores = [jnp.dot(q, kt[j], preferred_element_type=f32) for j in range(2)]
        peak = jnp.maximum(
            jnp.max(scores[0], axis=-1, keepdims=True), jnp.max(scores[1], axis=-1, keepdims=True)
        )
        total = jnp.zeros((block, 2 * hs), f32)
        for j in range(2):
            p = jnp.exp2(scores[j] - peak).astype(bf16)
            total += jnp.dot(p, vx[j], preferred_element_type=f32)
        oa[i] = total
        top[i] = jnp.broadcast_to(peak, (block, hs))

    for rel in (LEFT, RIGHT, OPP):
        outs.y_relay(rel)

    @pl.when(has_beside)
    def _():
        for n in names:
            copies.got("kv" + n)
        take(2, kvb[1].reshape(keys, 2 * hs))

    def attend(rx):
        @pl.when(has_beside)
        def _():
            @pl.loop(2 * rx, 2 * rx + 2)
            def _(i):
                s = jnp.dot(queries(i), kt[2], preferred_element_type=f32)
                old = top[i][:, :1]
                peak = jnp.maximum(old, jnp.max(s, axis=-1, keepdims=True))
                p = jnp.exp2(s - peak).astype(bf16)
                oa[i] = oa[i] * jnp.exp2(old - peak) + jnp.dot(
                    p, vx[2], preferred_element_type=f32
                )

        o = oa[2 * rx : 2 * rx + 2].reshape(2 * tokens, 2 * hs)
        attn = (o[:, :hs] / o[:, hs:]).astype(bf16).reshape(2, NZ, rows, hs)
        attn_g[rx, OWN] = attn[:, OWN].reshape(2 * rows, hs)
        for rz in (LEFT, RIGHT, OPP):
            attn_s[rx, rz] = attn[:, rz].reshape(2 * rows, hs)
            copies.start(
                f"t{rx}{rz}", attn_s.at[rx, rz], attn_g.at[rx, back[rz]], me.to(z=shift[rz])
            )

    def contribution(rx):
        copies.got(*[f"t{rx}{rz}" for rz in (LEFT, RIGHT, OPP)])
        a = jnp.concatenate([attn_g[rx, rz] for rz in range(NZ)], axis=-1)
        return jnp.dot(a, wo[...].reshape(NZ * hs, width), preferred_element_type=f32)

    attend(OPP)
    for rel in (LEFT, RIGHT, OPP):
        outs.y_end(rel)
    attend(RIGHT)
    attend(LEFT)
    own_wo.wait()
    for rel in (LEFT, RIGHT, OPP):
        outs.done(rel)

    sub = half // 2
    p = contribution(OPP).astype(bf16)
    for j in range(2):
        po[j] = p[:, j * sub : (j + 1) * sub]
        po[2 + j] = p[:, half + j * sub : half + (j + 1) * sub]
        copies.start(f"rl{j}", po.at[j], rl.at[j], me.to(x=1))
        copies.start(f"rr{j}", po.at[2 + j], rr.at[j], me.to(x=-1))
    attend(OWN)

    right = contribution(RIGHT)
    for j in range(2):
        pr_s[2 + j] = right[:, half + j * sub : half + (j + 1) * sub].astype(bf16)
        copies.start(f"fl{2 + j}", pr_s.at[2 + j], fl.at[2 + j], me.to(x=1))
    left = contribution(LEFT)
    for j in range(2):
        pl_s[j] = left[:, j * sub : (j + 1) * sub].astype(bf16)
        copies.start(f"fr{j}", pl_s.at[j], fr.at[j], me.to(x=-1))
    for j in range(2):
        copies.got(f"rl{j}")
        pr_s[j] = (right[:, j * sub : (j + 1) * sub] + rl[j].astype(f32)).astype(bf16)
        copies.start(f"fl{j}", pr_s.at[j], fl.at[j], me.to(x=1))
        copies.got(f"rr{j}")
        pl_s[2 + j] = (
            left[:, half + j * sub : half + (j + 1) * sub] + rr[j].astype(f32)
        ).astype(bf16)
        copies.start(f"fr{2 + j}", pl_s.at[2 + j], fr.at[2 + j], me.to(x=-1))

    p = contribution(OWN)
    copies.got("qs")
    qb[core] = queue_ref[core]
    gate = mods_ref[core, 2:3, :]
    sends_on = jnp.logical_and(core == 1, frame < frames - 1)
    near, next0, next1 = {}, {}, {}
    for j in range(2):
        copies.got(f"fl{j}", f"fr{j}", f"fl{2 + j}", f"fr{2 + j}")
        for h in (j, 2 + j):
            cols = slice(h * sub, (h + 1) * sub)
            proj = p[:, cols] + fl[h].astype(f32) + fr[h].astype(f32)
            for tok in range(2):
                ob[h, tok] = (
                    qb[tok, :, cols].astype(f32)
                    + gate[:, cols] * proj[tok * rows : (tok + 1) * rows]
                ).astype(bf16)
        for h in (j, 2 + j):
            near[h] = copies.make(f"o{h}", ob.at[h, 1], ou.at[1, h], me.to(flip=True))
            next0[h] = copies.make(f"n{h}", ob.at[h, 0], ou.at[0, h], (after, me.head, 0))
            next1[h] = pltpu.make_async_remote_copy(
                src_ref=ob.at[h, 1], dst_ref=ou.at[0, h],
                send_sem=local.at[2 + h], recv_sem=recv.at[copies.count - 1],
                device_id=(after, me.head, 1), device_id_type=MESH,
            )

        @pl.when(core == 0)
        def _():
            for h in (j, 2 + j):
                near[h].start()
                out_ref[1, :, h * sub : (h + 1) * sub] = ob[h, 0]

        @pl.when(sends_on)
        def _():
            for h in (j, 2 + j):
                next0[h].start()
                next1[h].start()

    @pl.when(frame == 0)
    def _():
        out_ref[0] = noise_ref[...]

    @pl.when(core == 1)
    def _():
        for h in range(4):
            near[h].wait_recv()
            out_ref[1, :, h * sub : (h + 1) * sub] = ou[1, h]

    @pl.when(frame > 0)
    def _():
        for h in range(4):
            next0[h].wait_recv()
            out_ref[0, :, h * sub : (h + 1) * sub] = ou[0, h]

    @pl.when(core == 0)
    def _():
        for h in range(4):
            near[h].wait_send()

    @pl.when(sends_on)
    def _():
        for h in range(4):
            next0[h].wait_send()
            next1[h].wait_send()

    @pl.when(has_beside)
    def _():
        for n in names:
            copies.all["kv" + n].wait_send()

    copies.sent(skip=[f"{t}{h}" for t in "on" for h in range(4)] + ["kv" + n for n in names])


def body(queue, timesteps, mod_table, w_qkv, norm_gains, w_out, noise_frame):
    slots, rows, width = queue.shape
    hs = w_out.shape[1]
    bf16, f32 = jnp.bfloat16, jnp.float32
    vmem = pl.BlockSpec(memory_space=pltpu.VMEM)
    hbm = pl.BlockSpec(memory_space=pl.ANY)
    tokens = NZ * rows
    keys = NX * 2 * tokens
    eighth = width // 8
    half = width // 2
    sub = half // 2
    mods = jnp.stack(
        [lax.dynamic_index_in_dim(mod_table, timesteps[i], 0, keepdims=False) for i in range(slots)]
    )
    return pl.pallas_call(
        block_kernel,
        out_shape=jax.ShapeDtypeStruct(queue.shape, bf16),
        in_specs=[vmem, vmem, vmem, vmem, hbm, hbm],
        out_specs=vmem,
        scratch_shapes=[
            pltpu.VMEM((NZ, 2 * rows, width), bf16),
            pltpu.VMEM((NX, 8, eighth, 3 * hs), bf16),
            pltpu.VMEM((NX, 2, NZ, rows, 3 * hs), bf16),
            pltpu.VMEM((NX * 2, NZ, rows, 3 * hs), bf16),
            pltpu.VMEM((2, NX * 2, NZ, rows, 2 * hs), bf16),
            pltpu.VMEM((3, hs, keys), bf16),
            pltpu.VMEM((3, keys, 2 * hs), bf16),
            pltpu.VMEM((NX * 2, tokens, 2 * hs), f32),
            pltpu.VMEM((NX * 2, tokens, hs), f32),
            pltpu.VMEM((NX, NZ, 2 * rows, hs), bf16),
            pltpu.VMEM((NX, NZ, 2 * rows, hs), bf16),
            pltpu.VMEM((NZ, 8, hs // 8, width), bf16),
            pltpu.VMEM((4, 2 * rows, sub), bf16),
            pltpu.VMEM((4, 2 * rows, sub), bf16),
            pltpu.VMEM((4, 2 * rows, sub), bf16),
            pltpu.VMEM((2, 2 * rows, sub), bf16),
            pltpu.VMEM((2, 2 * rows, sub), bf16),
            pltpu.VMEM((4, 2 * rows, sub), bf16),
            pltpu.VMEM((4, 2 * rows, sub), bf16),
            pltpu.VMEM((2, rows, width), bf16),
            pltpu.VMEM((4, 2, rows, sub), bf16),
            pltpu.VMEM((2, 4, rows, sub), bf16),
            pltpu.SemaphoreType.DMA((6,)),
            pltpu.SemaphoreType.DMA((160,)),
            pltpu.SemaphoreType.DMA((160,)),
        ],
        compiler_params=pltpu.CompilerParams(
            collective_id=0, has_side_effects=True, vmem_limit_bytes=56 * 1024 * 1024
        ),
        name="block",
    )(
        mods, queue, noise_frame, norm_gains,
        w_qkv.reshape(8, eighth, 3 * hs), w_out.reshape(8, hs // 8, width),
    )


def solution(mesh):
    return jax.shard_map(
        body,
        mesh=mesh,
        in_specs=(
            P("frame", ("head", "tok"), None),
            P("frame"),
            P(),
            P(None, "head", None),
            P(),
            P("head", None, None),
            P(("head", "tok"), None),
        ),
        out_specs=P("frame", ("head", "tok"), None),
        check_vma=False,
    )
```

time: 315 us -> 110 us (0.35)
  waiting for transfers between devices: 248 us -> 0 us
  Pallas kernels: 0 us -> 99.4 us
  matrix products: 19.4 us -> 0 us
  other arithmetic: 13.8 us -> 0.66 us
  between operations: 13.3 us -> 3.88 us
  starting transfers between devices: 7.71 us -> 0 us
  local copies, waits for them, and re-layouts: 8.51 us -> 4.24 us
    all_gather x2 -> x0, waiting for transfers between devices: 114 us -> none  [the longest x1 93.9 us: body(): lax.all_gather(modulated, 'head', axis=1, tiled=True)]
    reduce_scatter x1 -> x0, waiting for transfers between devices: 109 us -> none  [body(): lax.psum_scatter(lax.optimization_barrier(contrib.astype(jnp.bfloat16)).a...]
    pallas_call x0 -> x1, Pallas kernels: none -> 99.4 us  [body(): pl.pallas_call(block_kernel, out_shape=jax.ShapeDtypeStruct(queue.shape,...]
    ppermute x3 -> x0, waiting for transfers between devices: 25.8 us -> none  [the longest x1 13.1 us: padded(): lax.ppermute(head, axis, [((i + 1) % count, i) for i in range(ends)])]
    dot_general x7 -> x0, matrix products: 19.4 us -> none  [the longest x2 4.91 us: attend_rows(): lax.dot_general(queries, key_rows, (((1,), (1,)), ((), ())), preferred_el...]
    ppermute x3 -> x0, starting transfers between devices: 7.62 us -> none  [the longest x1 3.21 us: from_behind(): lax.ppermute(value, axis, [(source, source + steps) for source in range(f...]
    reduce_sum x5 -> x0, other arithmetic: 5.37 us -> none  [the longest x2 2.85 us: attend_rows(): total_p = jnp.sum(probs, axis=-1, keepdims=True)]
    concatenate x2 -> x0, local copies, waits for them, and re-layouts: 5.22 us -> none  [padded(): jnp.concatenate([lax.ppermute(tail, axis, [(i, (i + 1) % count) for i in...]
  transfers between devices with their start and end apart: 6 -> 0, of which waited for: 6 -> 0; matrix products, arithmetic and copies ran while one was open for 0% -> 0% of each run, Pallas kernels for 0% -> 0%
where the time goes in v2:
time: 110 us; the launch traced here: 108 us
  Pallas kernels  99.4 us (90%)
  local copies, waits for them, and re-layouts  4.24 us (4%)
  between operations  3.88 us (4%)
    pallas_call x1, Pallas kernels, body(): pl.pallas_call(block_kernel, out_shape=jax.ShapeDtypeStruct(queue.shape,...  99.4 us

profile of v2, /device:TPU:1, one launch (start us, length us, event | category | flops | bytes accessed | tf_op | source)
XLA Modules:
  0.0 108.2 jit_solution(14036983211080336634)
XLA Ops:
  0.0 1.3 %fusion = (s32[1]{0:T(128)}, s32[1]{0:T(128)}) fusion(s32[2]{0:T(128)} %param.8), kind=kLoop, calls=%fused_computation.3 | loop fusion | bytes 16 | tf_op jit(solution)/shard_map/slice | solution.py:504
  5.2 1.1 %constant_dynamic-slice_fusion.1 = (f32[1,3,3072]{2,0,1:T(1,128)S(1)}, f32[1,3,3072]{2,0,1:T(1,128)S(1)}) fusion(f32[50,3,3072]{2,0,1:T(8,128)} %param.9, s32[]{:T(128)S(6)} %select_n.7, s32[]{:T(128)S(6)} %select_n.8), kind=kLoop, calls=%fused_computation.2 | loop fusion | bytes 147464 | tf_op jit(solution)/shard_map/jit(dynamic_index_in_dim)/dynamic_slice | solution.py:504
  6.3 0.7 pad_maximum_fusion.mods_ref
  7.0 99.4 %block.1 = bf16[2,32,3072]{2,1,0:T(8,128)(2,1)} custom-call(f32[2,3,3072]{2,1,0:T(4,128)} %pad_maximum_fusion.mods_ref, bf16[2,32,3072]{2,1,0:T(8,128)(2,1)} %queue_ref.1, bf16[32,3072]{1,0:T(8,128)(2,1)} %noise_ref.1, f32[2,128]{1,0:T(2,128)} %gains_ref.1, bf16[8,384,384]{2,1,0:T(8,128)(2,1)} %bitcast.4, bf16[8,16,3072]{2,1,0:T(8,128)(2,1)} %bitcast.5), custom_call_target="tpu_custom_call" | custom-call | tf_op jit(solution)/shard_map/block/pallas_call | solution.py:506
  106.4 1.8 %copy.13 = bf16[2,32,3072]{2,1,0:T(8,128)(2,1)} copy(bf16[2,32,3072]{2,1,0:T(8,128)(2,1)} %block.1) | data formatting | bytes 786432
  (2 shorter events, 0.0 us)

commit v3 on v2

--- a/solution.py
+++ b/solution.py
@@ -137,8 +137,8 @@
 
 
 def block_kernel(
-    mods_ref, queue_ref, noise_ref, gains_ref, w_hbm, wo_hbm, out_ref,
-    xg, wg, sb, rb, kvb, kt, vx, oa, top, attn_s, attn_g, wo, po, pr_s, pl_s, rl, rr, fl, fr,
+    steps_ref, mod_hbm, queue_ref, noise_ref, gains_ref, w_hbm, wo_hbm, out_ref,
+    mod, xg, wg, sb, rb, kvb, kt, vx, oa, top, attn_s, attn_g, wo, po, pr_s, pl_s, rl, rr, fl, fr,
     qb, ob, ou, local, send, recv,
 ):
     me = Place()
@@ -157,6 +157,8 @@
     back = {LEFT: RIGHT, RIGHT: LEFT, OPP: OPP}
     shift = {LEFT: -1, RIGHT: 1, OPP: 2}
 
+    mod_copy = pltpu.make_async_copy(mod_hbm, mod, local.at[6])
+    mod_copy.start()
     own_w = pltpu.make_async_copy(w_hbm, wg.at[OWN], local.at[0])
     own_w.start()
     own_wo = pltpu.make_async_copy(wo_hbm, wo.at[OWN], local.at[1])
@@ -178,12 +180,22 @@
                 barrier, inc=1, device_id=(after, me.head, tok), device_id_type=MESH
             )
 
+    mod_copy.wait()
+    for slot in range(2):
+        level = pl.ds(steps_ref[slot], 1)
+        x = queue_ref[slot].astype(f32)
+        centred = x - jnp.mean(x, axis=-1, keepdims=True)
+        normed = centred * lax.rsqrt(jnp.mean(centred * centred, axis=-1, keepdims=True) + 1e-06)
+        xg[OWN, slot * rows : (slot + 1) * rows, :] = (
+            normed * (1.0 + mod[1, level, :]) + mod[0, level, :]
+        ).astype(bf16)
+
     pl.semaphore_wait(barrier, len(partners) + 2 * core)
 
     copies = Copies(send, recv)
     mine = me.core * NY + me.y
     seg = wg.shape[2]
-    direct = seg // 4 // 32 * 32
+    direct = seg // 3 // 32 * 32
     part = (seg - direct) // 2
     weights = Gather(
         "w", copies, me, "x", (lambda e: w_hbm.at[e, pl.ds(direct, 2 * part)]), wg,
@@ -196,17 +208,6 @@
     def rows_of(rel, first, count):
         return wg.at[rel, quad, pl.ds(first, count)]
 
-    source = w_hbm.at[quad, pl.ds(0, direct)]
-    copies.start("dr", source, rows_of(LEFT, 0, direct), me.to(x=1))
-    copies.start("dl", source, rows_of(RIGHT, 0, direct), me.to(x=-1))
-
-    for slot in range(2):
-        x = queue_ref[slot].astype(f32)
-        centred = x - jnp.mean(x, axis=-1, keepdims=True)
-        normed = centred * lax.rsqrt(jnp.mean(centred * centred, axis=-1, keepdims=True) + 1e-06)
-        xg[OWN, slot * rows : (slot + 1) * rows, :] = (
-            normed * (1.0 + mods_ref[slot, 1:2, :]) + mods_ref[slot, 0:1, :]
-        ).astype(bf16)
     first, second = pl.ds(0, rows), pl.ds(rows, rows)
     copies.start("zr0", xg.at[OWN, first], xg.at[LEFT, first], me.to(z=1))
     copies.start("zl1", xg.at[OWN, second], xg.at[RIGHT, second], me.to(z=-1))
@@ -215,11 +216,21 @@
     copies.start("qs", queue_ref.at[1 - core], qb.at[core], me.to(flip=True))
 
     weights.ring_relay()
-    weights.ring_end()
+    source = w_hbm.at[quad, pl.ds(0, direct)]
+    copies.start("dr", source, rows_of(LEFT, 0, direct), me.to(x=1))
+    copies.start("dl", source, rows_of(RIGHT, 0, direct), me.to(x=-1))
     copies.got("zr0")
     copies.start("zrr", xg.at[LEFT, first], xg.at[OPP, first], me.to(z=1))
     copies.got("zl1")
     copies.start("zll", xg.at[RIGHT, second], xg.at[OPP, second], me.to(z=-1))
+    outs = Gather(
+        "o", copies, me, "z", (lambda e: wo_hbm.at[e]), wo,
+        lambda ref, rel, e, which: ref.at[rel, e, :, pl.ds(which * half, half)],
+        lambda ref, rel, e: ref.at[rel, e],
+    )
+    outs.ring_start()
+    weights.ring_end()
+    weights.y_relay(LEFT)
     copies.got("dr")
     low, high = direct // 2, direct - direct // 2
     copies.start("drr", rows_of(LEFT, 0, low), rows_of(OPP, 0, low), me.to(x=1))
@@ -227,11 +238,7 @@
     copies.got("dl")
     copies.start("dll", rows_of(RIGHT, low, high), rows_of(OPP, low, high), me.to(x=-1))
     copies.start("ds2", rows_of(RIGHT, 0, direct), rows_of(RIGHT, 0, direct), me.to(flip=True))
-    weights.y_relay(LEFT)
     weights.y_relay(RIGHT)
-    weights.y_end(LEFT)
-    copies.got("drr", "dll")
-    copies.start("ds3", rows_of(OPP, 0, direct), rows_of(OPP, 0, direct), me.to(flip=True))
 
     q_gain = gains_ref[0:1, :] * f32(1.4426950408889634 / hs**0.5)
     k_gain = gains_ref[1:2, :]
@@ -281,34 +288,32 @@
     copies.got("zr1", "zl0")
     project(OWN, 0)
     weights.y_relay(OPP)
+    weights.y_end(LEFT)
     weights.done(LEFT)
     copies.got("ds1")
     project(LEFT, 0)
+    share(OWN, 0)
     weights.y_end(RIGHT)
     weights.done(RIGHT)
     copies.got("ds2")
     project(RIGHT, 0)
-    share(OWN, 0)
+    copies.got("drr", "dll")
+    copies.start("ds3", rows_of(OPP, 0, direct), rows_of(OPP, 0, direct), me.to(flip=True))
+    share(LEFT, 0)
+    weights.y_end(OPP)
     copies.got("zrr", "zll")
     project(OWN, 1)
     project(LEFT, 1)
     project(RIGHT, 1)
-    weights.y_end(OPP)
+    share(RIGHT, 0)
     weights.done(OPP)
     copies.got("ds3")
     project(OPP, 0)
     project(OPP, 1)
-    outs = Gather(
-        "o", copies, me, "z", (lambda e: wo_hbm.at[e]), wo,
-        lambda ref, rel, e, which: ref.at[rel, e, :, pl.ds(which * half, half)],
-        lambda ref, rel, e: ref.at[rel, e],
-    )
-    outs.ring_start()
-    share(LEFT, 0)
-    share(RIGHT, 0)
     share(OWN, 1)
     share(LEFT, 1)
     share(RIGHT, 1)
+    outs.ring_relay()
     share(OPP, 0)
     share(OPP, 1)
     names = [f"{rel}{group}" for rel in range(4) for group in range(2)]
@@ -321,17 +326,16 @@
         vx[which, :, hs:] = ones
 
     take(0, rb[...].reshape(keys, 3 * hs)[:, hs:])
-    outs.ring_relay()
+    outs.ring_end()
     copies.got(*["ks" + n for n in names])
     take(1, kvb[0].reshape(keys, 2 * hs))
-    outs.ring_end()
-
-    block = tokens
+
+    block = 2 * tokens
 
     def queries(i):
-        return rb[i].reshape(block, 3 * hs)[:, :hs]
-
-    @pl.loop(0, 2 * NX)
+        return rb[pl.ds(2 * i, 2)].reshape(block, 3 * hs)[:, :hs]
+
+    @pl.loop(0, NX)
     def _(i):
         q = queries(i)
         scores = [jnp.dot(q, kt[j], preferred_element_type=f32) for j in range(2)]
@@ -357,17 +361,15 @@
     def attend(rx):
         @pl.when(has_beside)
         def _():
-            @pl.loop(2 * rx, 2 * rx + 2)
-            def _(i):
-                s = jnp.dot(queries(i), kt[2], preferred_element_type=f32)
-                old = top[i][:, :1]
-                peak = jnp.maximum(old, jnp.max(s, axis=-1, keepdims=True))
-                p = jnp.exp2(s - peak).astype(bf16)
-                oa[i] = oa[i] * jnp.exp2(old - peak) + jnp.dot(
-                    p, vx[2], preferred_element_type=f32
-                )
-
-        o = oa[2 * rx : 2 * rx + 2].reshape(2 * tokens, 2 * hs)
+            s = jnp.dot(queries(rx), kt[2], preferred_element_type=f32)
+            old = top[rx][:, :1]
+            peak = jnp.maximum(old, jnp.max(s, axis=-1, keepdims=True))
+            p = jnp.exp2(s - peak).astype(bf16)
+            oa[rx] = oa[rx] * jnp.exp2(old - peak) + jnp.dot(
+                p, vx[2], preferred_element_type=f32
+            )
+
+        o = oa[rx]
         attn = (o[:, :hs] / o[:, hs:]).astype(bf16).reshape(2, NZ, rows, hs)
         attn_g[rx, OWN] = attn[:, OWN].reshape(2 * rows, hs)
         for rz in (LEFT, RIGHT, OPP):
@@ -420,7 +422,7 @@
     p = contribution(OWN)
     copies.got("qs")
     qb[core] = queue_ref[core]
-    gate = mods_ref[core, 2:3, :]
+    gate = mod[2, pl.ds(steps_ref[core], 1), :]
     sends_on = jnp.logical_and(core == 1, frame < frames - 1)
     near, next0, next1 = {}, {}, {}
     for j in range(2):
@@ -495,20 +497,20 @@
     bf16, f32 = jnp.bfloat16, jnp.float32
     vmem = pl.BlockSpec(memory_space=pltpu.VMEM)
     hbm = pl.BlockSpec(memory_space=pl.ANY)
+    smem = pl.BlockSpec(memory_space=pltpu.SMEM)
     tokens = NZ * rows
     keys = NX * 2 * tokens
     eighth = width // 8
     half = width // 2
     sub = half // 2
-    mods = jnp.stack(
-        [lax.dynamic_index_in_dim(mod_table, timesteps[i], 0, keepdims=False) for i in range(slots)]
-    )
+    table = jnp.transpose(mod_table, (1, 0, 2))
     return pl.pallas_call(
         block_kernel,
         out_shape=jax.ShapeDtypeStruct(queue.shape, bf16),
-        in_specs=[vmem, vmem, vmem, vmem, hbm, hbm],
+        in_specs=[smem, hbm, vmem, vmem, vmem, hbm, hbm],
         out_specs=vmem,
         scratch_shapes=[
+            pltpu.VMEM(table.shape, f32),
             pltpu.VMEM((NZ, 2 * rows, width), bf16),
             pltpu.VMEM((NX, 8, eighth, 3 * hs), bf16),
             pltpu.VMEM((NX, 2, NZ, rows, 3 * hs), bf16),
@@ -516,8 +518,8 @@
             pltpu.VMEM((2, NX * 2, NZ, rows, 2 * hs), bf16),
             pltpu.VMEM((3, hs, keys), bf16),
             pltpu.VMEM((3, keys, 2 * hs), bf16),
-            pltpu.VMEM((NX * 2, tokens, 2 * hs), f32),
-            pltpu.VMEM((NX * 2, tokens, hs), f32),
+            pltpu.VMEM((NX, 2 * tokens, 2 * hs), f32),
+            pltpu.VMEM((NX, 2 * tokens, hs), f32),
             pltpu.VMEM((NX, NZ, 2 * rows, hs), bf16),
             pltpu.VMEM((NX, NZ, 2 * rows, hs), bf16),
             pltpu.VMEM((NZ, 8, hs // 8, width), bf16),
@@ -531,7 +533,7 @@
             pltpu.VMEM((2, rows, width), bf16),
             pltpu.VMEM((4, 2, rows, sub), bf16),
             pltpu.VMEM((2, 4, rows, sub), bf16),
-            pltpu.SemaphoreType.DMA((6,)),
+            pltpu.SemaphoreType.DMA((7,)),
             pltpu.SemaphoreType.DMA((160,)),
             pltpu.SemaphoreType.DMA((160,)),
         ],
@@ -540,7 +542,7 @@
         ),
         name="block",
     )(
-        mods, queue, noise_frame, norm_gains,
+        timesteps, table, queue, noise_frame, norm_gains,
         w_qkv.reshape(8, eighth, 3 * hs), w_out.reshape(8, hs // 8, width),
     )
 

time: 110 us -> 95.5 us (0.87)
  Pallas kernels: 99.4 us -> 92.7 us
  between operations: 3.88 us -> 0.01 us
  local copies, waits for them, and re-layouts: 4.24 us -> 1.77 us
    pallas_call x1, Pallas kernels: 99.4 us -> 92.7 us  [body(): pl.pallas_call(block_kernel, out_shape=jax.ShapeDtypeStruct(queue.shape,...]
    slice x1 -> x0, local copies, waits for them, and re-layouts: 1.34 us -> none  [body(): timesteps[i]]
    dynamic_slice x1 -> x0, local copies, waits for them, and re-layouts: 1.11 us -> none  [body(): lax.dynamic_index_in_dim(mod_table, timesteps[i], 0, keepdims=False)]
where the time goes in v3:
time: 95.5 us; the launch traced here: 94.5 us
  Pallas kernels  92.7 us (97%)
  local copies, waits for them, and re-layouts  1.77 us (2%)
    pallas_call x1, Pallas kernels, body(): pl.pallas_call(block_kernel, out_shape=jax.ShapeDtypeStruct(queue.shape,...  92.7 us

profile of v3, /device:TPU:1, one launch (start us, length us, event | category | flops | bytes accessed | tf_op | source)
XLA Modules:
  0.0 94.5 jit_solution(6002493869868428548)
XLA Ops:
  0.0 92.7 %block.1 = bf16[2,32,3072]{2,1,0:T(8,128)(2,1)} custom-call(s32[2]{0:T(128)} %steps_ref.1, f32[3,50,3072]{2,1,0:T(8,128)} %bitcast.4, bf16[2,32,3072]{2,1,0:T(8,128)(2,1)} %queue_ref.1, bf16[32,3072]{1,0:T(8,128)(2,1)} %noise_ref.1, f32[2,128]{1,0:T(2,128)} %gains_ref.1, bf16[8,384,384]{2,1,0:T(8,128)(2,1)} %bitcast.3, bf16[8,16,3072]{2,1,0:T(8,128)(2,1)} %bitcast.5), custom_call_target="tpu_custom_call" | custom-call | tf_op jit(solution)/shard_map/block/pallas_call | solution.py:507
  92.7 1.8 %copy.9 = bf16[2,32,3072]{2,1,0:T(8,128)(2,1)} copy(bf16[2,32,3072]{2,1,0:T(8,128)(2,1)} %block.1) | data formatting | bytes 786432

commit v4 on v3

--- a/solution.py
+++ b/solution.py
@@ -132,13 +132,52 @@
         self.got("s0" + n, "s1" + n, "s2" + n, "s3" + n)
 
 
+class Direct:
+    def __init__(self, tag, copies, me, source, held, count, cols):
+        self.tag, self.copies, self.me, self.count, self.cols = tag, copies, me, count, cols
+        self.source, self.held = source, held
+        self.quad = pl.ds(me.core * NY, NY)
+        self.low = count // 2
+
+    def rows(self, rel, first, count):
+        return self.held.at[rel, self.quad, pl.ds(first, count), self.cols]
+
+    def go(self, name, src, dst, device):
+        self.copies.start(self.tag + name, src, dst, device)
+
+    def got(self, *names):
+        self.copies.got(*[self.tag + name for name in names])
+
+    def start(self):
+        source = self.source.at[self.quad, pl.ds(0, self.count), self.cols]
+        self.go("r", source, self.rows(LEFT, 0, self.count), self.me.to(x=1))
+        self.go("l", source, self.rows(RIGHT, 0, self.count), self.me.to(x=-1))
+
+    def beside(self, rel):
+        part = self.rows(rel, 0, self.count)
+        self.go("s" + str(rel), part, part, self.me.to(flip=True))
+
+    def relay(self):
+        low, high = self.low, self.count - self.low
+        self.got("r")
+        self.go("rr", self.rows(LEFT, 0, low), self.rows(OPP, 0, low), self.me.to(x=1))
+        self.beside(LEFT)
+        self.got("l")
+        self.go("ll", self.rows(RIGHT, low, high), self.rows(OPP, low, high), self.me.to(x=-1))
+        self.beside(RIGHT)
+
+    def end(self):
+        self.got("rr", "ll")
+        self.beside(OPP)
+
+
 def rms_scale(values, gain):
     return values * lax.rsqrt(jnp.mean(values * values, axis=-1, keepdims=True) + 1e-06) * gain
 
 
 def block_kernel(
-    steps_ref, mod_hbm, queue_ref, noise_ref, gains_ref, w_hbm, wo_hbm, out_ref,
-    mod, xg, wg, sb, rb, kvb, kt, vx, oa, top, attn_s, attn_g, wo, po, pr_s, pl_s, rl, rr, fl, fr,
+    steps_ref, mod_hbm, queue_hbm, noise_hbm, gains_hbm, w_hbm, wo_hbm, out_hbm,
+    mod, queue_ref, gains_ref, xg, wg, sbk, rbk, sbq, rbq, kvb, kt, vx, oa, top, attn_s, attn_g, wo, po, pr_s, pl_s, rl, rr, fl, fr,
     qb, ob, ou, local, send, recv,
 ):
     me = Place()
@@ -159,11 +198,10 @@
 
     mod_copy = pltpu.make_async_copy(mod_hbm, mod, local.at[6])
     mod_copy.start()
-    own_w = pltpu.make_async_copy(w_hbm, wg.at[OWN], local.at[0])
-    own_w.start()
-    own_wo = pltpu.make_async_copy(wo_hbm, wo.at[OWN], local.at[1])
-    own_wo.start()
-
+    queue_copy = pltpu.make_async_copy(queue_hbm, queue_ref, local.at[7])
+    queue_copy.start()
+    gains_copy = pltpu.make_async_copy(gains_hbm, gains_ref, local.at[8])
+    gains_copy.start()
     partners = [me.to(flip=True)]
     for step in (1, -1, 2):
         partners += [me.to(x=step), me.to(x=step, flip=True), me.to(z=step)]
@@ -180,6 +218,7 @@
                 barrier, inc=1, device_id=(after, me.head, tok), device_id_type=MESH
             )
 
+    queue_copy.wait()
     mod_copy.wait()
     for slot in range(2):
         level = pl.ds(steps_ref[slot], 1)
@@ -189,36 +228,39 @@
         xg[OWN, slot * rows : (slot + 1) * rows, :] = (
             normed * (1.0 + mod[1, level, :]) + mod[0, level, :]
         ).astype(bf16)
-
     pl.semaphore_wait(barrier, len(partners) + 2 * core)
 
     copies = Copies(send, recv)
-    mine = me.core * NY + me.y
-    seg = wg.shape[2]
-    direct = seg // 3 // 32 * 32
-    part = (seg - direct) // 2
-    weights = Gather(
-        "w", copies, me, "x", (lambda e: w_hbm.at[e, pl.ds(direct, 2 * part)]), wg,
-        lambda ref, rel, e, which: ref.at[rel, e, pl.ds(direct + which * part, part)],
-        lambda ref, rel, e: ref.at[rel, e, pl.ds(direct, 2 * part)],
-    )
-    weights.ring_start()
-    quad = pl.ds(core * NY, NY)
-
-    def rows_of(rel, first, count):
-        return wg.at[rel, quad, pl.ds(first, count)]
-
+    rows_in = wg.shape[2]
+    direct = rows_in // 3 // 32 * 32
+    part = (rows_in - direct) // 2
+
+    def gather(tag, cols):
+        return Gather(
+            tag, copies, me, "x", (lambda e: w_hbm.at[e, pl.ds(direct, 2 * part), cols]), wg,
+            lambda ref, rel, e, which: ref.at[rel, e, pl.ds(direct + which * part, part), cols],
+            lambda ref, rel, e: ref.at[rel, e, pl.ds(direct, 2 * part), cols],
+        )
+
+    q_cols, kv_cols = pl.ds(0, hs), pl.ds(hs, 2 * hs)
+    wk, wq = gather("wk", kv_cols), gather("wq", q_cols)
+    dk = Direct("dk", copies, me, w_hbm, wg, direct, kv_cols)
+    dq = Direct("dq", copies, me, w_hbm, wg, direct, q_cols)
+    wk.ring_start()
+    own_w = pltpu.make_async_copy(w_hbm, wg.at[OWN], local.at[0])
+    own_w.start()
+    own_wo = pltpu.make_async_copy(wo_hbm, wo.at[OWN], local.at[1])
+    own_wo.start()
     first, second = pl.ds(0, rows), pl.ds(rows, rows)
     copies.start("zr0", xg.at[OWN, first], xg.at[LEFT, first], me.to(z=1))
     copies.start("zl1", xg.at[OWN, second], xg.at[RIGHT, second], me.to(z=-1))
     copies.start("zr1", xg.at[OWN, second], xg.at[LEFT, second], me.to(z=1))
     copies.start("zl0", xg.at[OWN, first], xg.at[RIGHT, first], me.to(z=-1))
-    copies.start("qs", queue_ref.at[1 - core], qb.at[core], me.to(flip=True))
-
-    weights.ring_relay()
-    source = w_hbm.at[quad, pl.ds(0, direct)]
-    copies.start("dr", source, rows_of(LEFT, 0, direct), me.to(x=1))
-    copies.start("dl", source, rows_of(RIGHT, 0, direct), me.to(x=-1))
+    copies.start("qs", queue_hbm.at[1 - core], qb.at[core], me.to(flip=True))
+
+    wk.ring_relay()
+    dk.start()
+    wq.ring_start()
     copies.got("zr0")
     copies.start("zrr", xg.at[LEFT, first], xg.at[OPP, first], me.to(z=1))
     copies.got("zl1")
@@ -229,54 +271,65 @@
         lambda ref, rel, e: ref.at[rel, e],
     )
     outs.ring_start()
-    weights.ring_end()
-    weights.y_relay(LEFT)
-    copies.got("dr")
-    low, high = direct // 2, direct - direct // 2
-    copies.start("drr", rows_of(LEFT, 0, low), rows_of(OPP, 0, low), me.to(x=1))
-    copies.start("ds1", rows_of(LEFT, 0, direct), rows_of(LEFT, 0, direct), me.to(flip=True))
-    copies.got("dl")
-    copies.start("dll", rows_of(RIGHT, low, high), rows_of(OPP, low, high), me.to(x=-1))
-    copies.start("ds2", rows_of(RIGHT, 0, direct), rows_of(RIGHT, 0, direct), me.to(flip=True))
-    weights.y_relay(RIGHT)
-
+    wk.ring_end()
+    wk.y_relay(LEFT)
+    wk.y_relay(RIGHT)
+    dk.relay()
+    wq.ring_relay()
+    dq.start()
+    wk.y_relay(OPP)
+    wk.y_end(LEFT)
+    wk.y_end(RIGHT)
+    dk.end()
+    gains_copy.wait()
     q_gain = gains_ref[0:1, :] * f32(1.4426950408889634 / hs**0.5)
     k_gain = gains_ref[1:2, :]
     groups = (pl.ds(0, NZ - 1), pl.ds(NZ - 1, 1))
     sizes = (NZ - 1, 1)
 
-    def project(rel, group):
+    def send_rows(tag, sent, home, rel, which):
+        if rel == OWN:
+            copies.start(
+                "a" + tag, sent.at[OWN, 1 - core, which], home.at[core, which], me.to(flip=True)
+            )
+            home[core, which] = sent[OWN, core, which]
+            return
+        spot = home.at[back[rel] * 2 + core, which]
+        copies.start("a" + tag, sent.at[rel, core, which], spot, me.to(x=shift[rel]))
+        copies.start(
+            "b" + tag, sent.at[rel, 1 - core, which], spot, me.to(x=shift[rel], flip=True)
+        )
+
+    def project_kv(rel, group):
         which, count = groups[group], sizes[group]
         xs = xg[which].reshape(count * 2 * rows, width)
-        w = wg[rel].reshape(width, 3 * hs)
-        qkv = jnp.dot(xs, w, preferred_element_type=f32)
-        q = rms_scale(qkv[:, :hs], q_gain)
-        k = rms_scale(qkv[:, hs : 2 * hs], k_gain)
-        out = jnp.concatenate([q, k, qkv[:, 2 * hs :]], axis=-1).astype(bf16)
-        out = out.reshape(count, 2, rows, 3 * hs)
+        w = wg[rel, :, :, hs:].reshape(width, 2 * hs)
+        kv = jnp.dot(xs, w, preferred_element_type=f32)
+        k = rms_scale(kv[:, :hs], k_gain)
+        out = jnp.concatenate([k, kv[:, hs:]], axis=-1).astype(bf16)
+        out = out.reshape(count, 2, rows, 2 * hs)
         for slot in range(2):
-            sb[rel, slot, which] = out[:, slot]
-        n = f"{rel}{group}"
-        if rel == OWN:
-            copies.start(
-                "a" + n, sb.at[OWN, 1 - core, which], rb.at[core, which], me.to(flip=True)
-            )
-            rb[core, which] = sb[OWN, core, which]
-            return
-        spot = rb.at[back[rel] * 2 + core, which]
-        copies.start("a" + n, sb.at[rel, core, which], spot, me.to(x=shift[rel]))
-        copies.start("b" + n, sb.at[rel, 1 - core, which], spot, me.to(x=shift[rel], flip=True))
+            sbk[rel, slot, which] = out[:, slot]
+        send_rows(f"k{rel}{group}", sbk, rbk, rel, which)
+
+    def project_q(rel):
+        xs = xg[...].reshape(NZ * 2 * rows, width)
+        w = wg[rel, :, :, :hs].reshape(width, hs)
+        q = rms_scale(jnp.dot(xs, w, preferred_element_type=f32), q_gain)
+        out = q.astype(bf16).reshape(NZ, 2, rows, hs)
+        for slot in range(2):
+            sbq[rel, slot] = out[:, slot]
+        send_rows(f"q{rel}", sbq, rbq, rel, pl.ds(0, NZ))
 
     def share(rel, group):
         n = f"{rel}{group}"
-        copies.got("a" + n)
+        copies.got("ak" + n)
         if rel != OWN:
-            copies.got("b" + n)
+            copies.got("bk" + n)
         spot = OWN if rel == OWN else back[rel]
         pair = pl.ds(spot * 2, 2)
-        src = rb.at[pair, groups[group], :, pl.ds(hs, 2 * hs)]
-        dst = kvb.at[1, pair, groups[group]]
-        side = copies.make("kv" + n, src, dst, (beside, me.head, 1 - core))
+        src = rbk.at[pair, groups[group]]
+        side = copies.make("kv" + n, src, kvb.at[1, pair, groups[group]], (beside, me.head, 1 - core))
 
         @pl.when(has_beside)
         def _():
@@ -286,35 +339,47 @@
 
     own_w.wait()
     copies.got("zr1", "zl0")
-    project(OWN, 0)
-    weights.y_relay(OPP)
-    weights.y_end(LEFT)
-    weights.done(LEFT)
-    copies.got("ds1")
-    project(LEFT, 0)
+    project_kv(OWN, 0)
+    wq.ring_end()
+    wk.done(LEFT)
+    dk.got("s1")
+    project_kv(LEFT, 0)
+    wk.done(RIGHT)
+    dk.got("s2")
+    project_kv(RIGHT, 0)
     share(OWN, 0)
-    weights.y_end(RIGHT)
-    weights.done(RIGHT)
-    copies.got("ds2")
-    project(RIGHT, 0)
-    copies.got("drr", "dll")
-    copies.start("ds3", rows_of(OPP, 0, direct), rows_of(OPP, 0, direct), me.to(flip=True))
+    wk.y_end(OPP)
+    wq.y_relay(LEFT)
+    dq.relay()
+    wk.done(OPP)
+    dk.got("s3")
+    project_kv(OPP, 0)
+    wq.y_relay(RIGHT)
     share(LEFT, 0)
-    weights.y_end(OPP)
+    share(RIGHT, 0)
+    wq.y_relay(OPP)
+    wq.y_end(LEFT)
     copies.got("zrr", "zll")
-    project(OWN, 1)
-    project(LEFT, 1)
-    project(RIGHT, 1)
-    share(RIGHT, 0)
-    weights.done(OPP)
-    copies.got("ds3")
-    project(OPP, 0)
-    project(OPP, 1)
-    share(OWN, 1)
-    share(LEFT, 1)
-    share(RIGHT, 1)
+    for rel in range(4):
+        project_kv(rel, 1)
     outs.ring_relay()
     share(OPP, 0)
+    dq.end()
+    wq.y_end(RIGHT)
+    wq.y_end(OPP)
+    project_q(OWN)
+    share(OWN, 1)
+    wq.done(LEFT)
+    dq.got("s1")
+    project_q(LEFT)
+    share(LEFT, 1)
+    wq.done(RIGHT)
+    dq.got("s2")
+    project_q(RIGHT)
+    share(RIGHT, 1)
+    wq.done(OPP)
+    dq.got("s3")
+    project_q(OPP)
     share(OPP, 1)
     names = [f"{rel}{group}" for rel in range(4) for group in range(2)]
 
@@ -325,7 +390,7 @@
         vx[which, :, :hs] = kv[:, hs:]
         vx[which, :, hs:] = ones
 
-    take(0, rb[...].reshape(keys, 3 * hs)[:, hs:])
+    take(0, rbk[...].reshape(keys, 2 * hs))
     outs.ring_end()
     copies.got(*["ks" + n for n in names])
     take(1, kvb[0].reshape(keys, 2 * hs))
@@ -333,11 +398,10 @@
     block = 2 * tokens
 
     def queries(i):
-        return rb[pl.ds(2 * i, 2)].reshape(block, 3 * hs)[:, :hs]
-
-    @pl.loop(0, NX)
-    def _(i):
-        q = queries(i)
+        return rbq[pl.ds(2 * i, 2)].reshape(block, hs)
+
+    def first_part(rx):
+        q = queries(rx)
         scores = [jnp.dot(q, kt[j], preferred_element_type=f32) for j in range(2)]
         peak = jnp.maximum(
             jnp.max(scores[0], axis=-1, keepdims=True), jnp.max(scores[1], axis=-1, keepdims=True)
@@ -346,17 +410,8 @@
         for j in range(2):
             p = jnp.exp2(scores[j] - peak).astype(bf16)
             total += jnp.dot(p, vx[j], preferred_element_type=f32)
-        oa[i] = total
-        top[i] = jnp.broadcast_to(peak, (block, hs))
-
-    for rel in (LEFT, RIGHT, OPP):
-        outs.y_relay(rel)
-
-    @pl.when(has_beside)
-    def _():
-        for n in names:
-            copies.got("kv" + n)
-        take(2, kvb[1].reshape(keys, 2 * hs))
+        oa[rx] = total
+        top[rx] = jnp.broadcast_to(peak, (block, hs))
 
     def attend(rx):
         @pl.when(has_beside)
@@ -383,11 +438,27 @@
         a = jnp.concatenate([attn_g[rx, rz] for rz in range(NZ)], axis=-1)
         return jnp.dot(a, wo[...].reshape(NZ * hs, width), preferred_element_type=f32)
 
+    copies.got("aq0")
+    for rel in (LEFT, RIGHT, OPP):
+        copies.got(f"aq{rel}", f"bq{rel}")
+    first_part(OPP)
+    first_part(RIGHT)
+    first_part(LEFT)
+    first_part(OWN)
+    for rel in (LEFT, RIGHT, OPP):
+        outs.y_relay(rel)
+
+    @pl.when(has_beside)
+    def _():
+        for n in names:
+            copies.got("kv" + n)
+        take(2, kvb[1].reshape(keys, 2 * hs))
+
     attend(OPP)
+    attend(RIGHT)
+    attend(LEFT)
     for rel in (LEFT, RIGHT, OPP):
         outs.y_end(rel)
-    attend(RIGHT)
-    attend(LEFT)
     own_wo.wait()
     for rel in (LEFT, RIGHT, OPP):
         outs.done(rel)
@@ -424,7 +495,13 @@
     qb[core] = queue_ref[core]
     gate = mod[2, pl.ds(steps_ref[core], 1), :]
     sends_on = jnp.logical_and(core == 1, frame < frames - 1)
-    near, next0, next1 = {}, {}, {}
+    near, next0, next1, kept = {}, {}, {}, {}
+    noise_copy = pltpu.make_async_copy(noise_hbm, out_hbm.at[0], local.at[9])
+
+    @pl.when(frame == 0)
+    def _():
+        noise_copy.start()
+
     for j in range(2):
         copies.got(f"fl{j}", f"fr{j}", f"fl{2 + j}", f"fr{2 + j}")
         for h in (j, 2 + j):
@@ -436,6 +513,8 @@
                     + gate[:, cols] * proj[tok * rows : (tok + 1) * rows]
                 ).astype(bf16)
         for h in (j, 2 + j):
+            cols = pl.ds(h * sub, sub)
+            kept[h] = pltpu.make_async_copy(ob.at[h, 0], out_hbm.at[1, :, cols], local.at[10 + h])
             near[h] = copies.make(f"o{h}", ob.at[h, 1], ou.at[1, h], me.to(flip=True))
             next0[h] = copies.make(f"n{h}", ob.at[h, 0], ou.at[0, h], (after, me.head, 0))
             next1[h] = pltpu.make_async_remote_copy(
@@ -448,7 +527,7 @@
         def _():
             for h in (j, 2 + j):
                 near[h].start()
-                out_ref[1, :, h * sub : (h + 1) * sub] = ob[h, 0]
+                kept[h].start()
 
         @pl.when(sends_on)
         def _():
@@ -456,26 +535,43 @@
                 next0[h].start()
                 next1[h].start()
 
-    @pl.when(frame == 0)
-    def _():
-        out_ref[0] = noise_ref[...]
+    def keep(slot, h):
+        cols = pl.ds(h * sub, sub)
+        return pltpu.make_async_copy(
+            ou.at[slot, h], out_hbm.at[slot, :, cols], local.at[14 + 4 * slot + h]
+        )
 
     @pl.when(core == 1)
     def _():
         for h in range(4):
             near[h].wait_recv()
-            out_ref[1, :, h * sub : (h + 1) * sub] = ou[1, h]
+            keep(1, h).start()
 
     @pl.when(frame > 0)
     def _():
         for h in range(4):
             next0[h].wait_recv()
-            out_ref[0, :, h * sub : (h + 1) * sub] = ou[0, h]
+            keep(0, h).start()
 
     @pl.when(core == 0)
     def _():
         for h in range(4):
             near[h].wait_send()
+            kept[h].wait()
+
+    @pl.when(core == 1)
+    def _():
+        for h in range(4):
+            keep(1, h).wait()
+
+    @pl.when(frame > 0)
+    def _():
+        for h in range(4):
+            keep(0, h).wait()
+
+    @pl.when(frame == 0)
+    def _():
+        noise_copy.wait()
 
     @pl.when(sends_on)
     def _():
@@ -495,7 +591,6 @@
     slots, rows, width = queue.shape
     hs = w_out.shape[1]
     bf16, f32 = jnp.bfloat16, jnp.float32
-    vmem = pl.BlockSpec(memory_space=pltpu.VMEM)
     hbm = pl.BlockSpec(memory_space=pl.ANY)
     smem = pl.BlockSpec(memory_space=pltpu.SMEM)
     tokens = NZ * rows
@@ -507,14 +602,18 @@
     return pl.pallas_call(
         block_kernel,
         out_shape=jax.ShapeDtypeStruct(queue.shape, bf16),
-        in_specs=[smem, hbm, vmem, vmem, vmem, hbm, hbm],
-        out_specs=vmem,
+        in_specs=[smem] + [hbm] * 6,
+        out_specs=hbm,
         scratch_shapes=[
             pltpu.VMEM(table.shape, f32),
+            pltpu.VMEM(queue.shape, bf16),
+            pltpu.VMEM(norm_gains.shape, f32),
             pltpu.VMEM((NZ, 2 * rows, width), bf16),
             pltpu.VMEM((NX, 8, eighth, 3 * hs), bf16),
-            pltpu.VMEM((NX, 2, NZ, rows, 3 * hs), bf16),
-            pltpu.VMEM((NX * 2, NZ, rows, 3 * hs), bf16),
+            pltpu.VMEM((NX, 2, NZ, rows, 2 * hs), bf16),
+            pltpu.VMEM((NX * 2, NZ, rows, 2 * hs), bf16),
+            pltpu.VMEM((NX, 2, NZ, rows, hs), bf16),
+            pltpu.VMEM((NX * 2, NZ, rows, hs), bf16),
             pltpu.VMEM((2, NX * 2, NZ, rows, 2 * hs), bf16),
             pltpu.VMEM((3, hs, keys), bf16),
             pltpu.VMEM((3, keys, 2 * hs), bf16),
@@ -533,9 +632,9 @@
             pltpu.VMEM((2, rows, width), bf16),
             pltpu.VMEM((4, 2, rows, sub), bf16),
             pltpu.VMEM((2, 4, rows, sub), bf16),
-            pltpu.SemaphoreType.DMA((7,)),
-            pltpu.SemaphoreType.DMA((160,)),
-            pltpu.SemaphoreType.DMA((160,)),
+            pltpu.SemaphoreType.DMA((22,)),
+            pltpu.SemaphoreType.DMA((200,)),
+            pltpu.SemaphoreType.DMA((200,)),
         ],
         compiler_params=pltpu.CompilerParams(
             collective_id=0, has_side_effects=True, vmem_limit_bytes=56 * 1024 * 1024

time: 95.5 us -> 92.3 us (0.966)
  Pallas kernels: 92.7 us -> 90.1 us
    pallas_call x1, Pallas kernels: 92.7 us -> 90.1 us  [body(): pl.pallas_call(block_kernel, out_shape=jax.ShapeDtypeStruct(queue.shape,...]
where the time goes in v4:
time: 92.3 us; the launch traced here: 91.8 us
  Pallas kernels  90.1 us (98%)
  local copies, waits for them, and re-layouts  1.77 us (2%)
    pallas_call x1, Pallas kernels, body(): pl.pallas_call(block_kernel, out_shape=jax.ShapeDtypeStruct(queue.shape,...  90.1 us

profile of v4, /device:TPU:1, one launch (start us, length us, event | category | flops | bytes accessed | tf_op | source)
XLA Modules:
  0.0 91.8 jit_solution(12294219387764375488)
XLA Ops:
  0.0 90.1 %block.1 = bf16[2,32,3072]{2,1,0:T(8,128)(2,1)} custom-call(s32[2]{0:T(128)} %steps_ref.1, f32[3,50,3072]{2,1,0:T(8,128)} %bitcast.4, bf16[2,32,3072]{2,1,0:T(8,128)(2,1)} %queue_hbm.1, bf16[32,3072]{1,0:T(8,128)(2,1)} %noise_hbm.1, f32[2,128]{1,0:T(2,128)} %gains_hbm.1, bf16[8,384,384]{2,1,0:T(8,128)(2,1)} %bitcast.3, bf16[8,16,3072]{2,1,0:T(8,128)(2,1)} %bitcast.5), custom_call_target="tpu_custom_call" | custom-call | tf_op jit(solution)/shard_map/block/pallas_call | solution.py:602
  90.1 1.8 %copy.9 = bf16[2,32,3072]{2,1,0:T(8,128)(2,1)} copy(bf16[2,32,3072]{2,1,0:T(8,128)(2,1)} %block.1) | data formatting | bytes 786432

commit v5 on v4

--- a/solution.py
+++ b/solution.py
@@ -130,6 +130,37 @@
     def done(self, rel):
         n = str(rel)
         self.got("s0" + n, "s1" + n, "s2" + n, "s3" + n)
+
+
+class PairGather(Gather):
+    def __init__(self, *args):
+        super().__init__(*args)
+        me = self.me
+        twin = me.y * 2 + 1 - me.zl
+        step = 2 * me.zl - 1
+        self.twin = (twin, me.head, me.core)
+        self.hop = (twin, me.x * NZ + (me.zh + step + NZ) % NZ, me.core)
+        self.got_first, self.got_second = 1 + me.zl, 2 - me.zl
+
+    def ring_start(self):
+        e = self.mine
+        self.go("r", self.source(e), self.whole(self.held, self.got_second, e), self.hop)
+
+    def ring_relay(self):
+        self.got("r")
+        part = self.whole(self.held, self.got_first, self.mine)
+        self.go("x", part, part, self.twin)
+
+    def ring_last(self):
+        e = self.mine
+        self.got("x")
+        self.go("rr", self.whole(self.held, self.got_second, e), self.whole(self.held, OPP, e), self.hop)
+        self.y_start(LEFT)
+        self.y_start(RIGHT)
+
+    def ring_end(self):
+        self.got("rr")
+        self.y_start(OPP)
 
 
 class Direct:
@@ -202,11 +233,17 @@
     queue_copy.start()
     gains_copy = pltpu.make_async_copy(gains_hbm, gains_ref, local.at[8])
     gains_copy.start()
+    copies = Copies(send, recv)
+    outs = PairGather(
+        "o", copies, me, "z", (lambda e: wo_hbm.at[e]), wo,
+        lambda ref, rel, e, which: ref.at[rel, e, :, pl.ds(which * half, half)],
+        lambda ref, rel, e: ref.at[rel, e],
+    )
     partners = [me.to(flip=True)]
     for step in (1, -1, 2):
         partners += [me.to(x=step), me.to(x=step, flip=True), me.to(z=step)]
     partners += [me.to(y=1), me.to(y=-1)]
-    partners += [(before, me.head, 1)]
+    partners += [(before, me.head, 1), outs.twin, outs.hop]
     barrier = pltpu.get_barrier_semaphore()
     for device in partners:
         pl.semaphore_signal(barrier, inc=1, device_id=device, device_id_type=MESH)
@@ -230,22 +267,22 @@
         ).astype(bf16)
     pl.semaphore_wait(barrier, len(partners) + 2 * core)
 
-    copies = Copies(send, recv)
     rows_in = wg.shape[2]
-    direct = rows_in // 3 // 32 * 32
-    part = (rows_in - direct) // 2
-
-    def gather(tag, cols):
-        return Gather(
-            tag, copies, me, "x", (lambda e: w_hbm.at[e, pl.ds(direct, 2 * part), cols]), wg,
+
+    q_cols, kv_cols = pl.ds(0, hs), pl.ds(hs, 2 * hs)
+
+    def gather(tag, cols, direct):
+        part = (rows_in - direct) // 2
+        ringed = Gather(
+            "w" + tag, copies, me, "x",
+            (lambda e: w_hbm.at[e, pl.ds(direct, 2 * part), cols]), wg,
             lambda ref, rel, e, which: ref.at[rel, e, pl.ds(direct + which * part, part), cols],
             lambda ref, rel, e: ref.at[rel, e, pl.ds(direct, 2 * part), cols],
         )
-
-    q_cols, kv_cols = pl.ds(0, hs), pl.ds(hs, 2 * hs)
-    wk, wq = gather("wk", kv_cols), gather("wq", q_cols)
-    dk = Direct("dk", copies, me, w_hbm, wg, direct, kv_cols)
-    dq = Direct("dq", copies, me, w_hbm, wg, direct, q_cols)
+        return ringed, Direct("d" + tag, copies, me, w_hbm, wg, direct, cols)
+
+    wk, dk = gather("k", kv_cols, rows_in * 5 // 12)
+    wq, dq = gather("q", q_cols, rows_in // 2)
     wk.ring_start()
     own_w = pltpu.make_async_copy(w_hbm, wg.at[OWN], local.at[0])
     own_w.start()
@@ -265,11 +302,6 @@
     copies.start("zrr", xg.at[LEFT, first], xg.at[OPP, first], me.to(z=1))
     copies.got("zl1")
     copies.start("zll", xg.at[RIGHT, second], xg.at[OPP, second], me.to(z=-1))
-    outs = Gather(
-        "o", copies, me, "z", (lambda e: wo_hbm.at[e]), wo,
-        lambda ref, rel, e, which: ref.at[rel, e, :, pl.ds(which * half, half)],
-        lambda ref, rel, e: ref.at[rel, e],
-    )
     outs.ring_start()
     wk.ring_end()
     wk.y_relay(LEFT)
@@ -347,6 +379,7 @@
     wk.done(RIGHT)
     dk.got("s2")
     project_kv(RIGHT, 0)
+    outs.ring_relay()
     share(OWN, 0)
     wk.y_end(OPP)
     wq.y_relay(LEFT)
@@ -362,8 +395,8 @@
     copies.got("zrr", "zll")
     for rel in range(4):
         project_kv(rel, 1)
-    outs.ring_relay()
     share(OPP, 0)
+    outs.ring_last()
     dq.end()
     wq.y_end(RIGHT)
     wq.y_end(OPP)
@@ -381,6 +414,7 @@
     dq.got("s3")
     project_q(OPP)
     share(OPP, 1)
+    outs.ring_end()
     names = [f"{rel}{group}" for rel in range(4) for group in range(2)]
 
     ones = jnp.ones((keys, hs), bf16)
@@ -389,11 +423,6 @@
         kt[which] = kv[:, :hs].T
         vx[which, :, :hs] = kv[:, hs:]
         vx[which, :, hs:] = ones
-
-    take(0, rbk[...].reshape(keys, 2 * hs))
-    outs.ring_end()
-    copies.got(*["ks" + n for n in names])
-    take(1, kvb[0].reshape(keys, 2 * hs))
 
     block = 2 * tokens
 
@@ -438,15 +467,19 @@
         a = jnp.concatenate([attn_g[rx, rz] for rz in range(NZ)], axis=-1)
         return jnp.dot(a, wo[...].reshape(NZ * hs, width), preferred_element_type=f32)
 
+    take(0, rbk[...].reshape(keys, 2 * hs))
+    copies.got(*["ks" + n for n in names])
+    take(1, kvb[0].reshape(keys, 2 * hs))
     copies.got("aq0")
     for rel in (LEFT, RIGHT, OPP):
         copies.got(f"aq{rel}", f"bq{rel}")
     first_part(OPP)
     first_part(RIGHT)
+    outs.y_relay(LEFT)
+    outs.y_relay(RIGHT)
     first_part(LEFT)
     first_part(OWN)
-    for rel in (LEFT, RIGHT, OPP):
-        outs.y_relay(rel)
+    outs.y_relay(OPP)
 
     @pl.when(has_beside)
     def _():
@@ -456,9 +489,9 @@
 
     attend(OPP)
     attend(RIGHT)
-    attend(LEFT)
     for rel in (LEFT, RIGHT, OPP):
         outs.y_end(rel)
+    attend(LEFT)
     own_wo.wait()
     for rel in (LEFT, RIGHT, OPP):
         outs.done(rel)

time: 92.3 us -> 89.6 us (0.971)
  Pallas kernels: 90.1 us -> 86.6 us
    pallas_call x1, Pallas kernels: 90.1 us -> 86.6 us  [body(): pl.pallas_call(block_kernel, out_shape=jax.ShapeDtypeStruct(queue.shape,...]
where the time goes in v5:
time: 89.6 us; the launch traced here: 88.3 us
  Pallas kernels  86.6 us (97%)
  local copies, waits for them, and re-layouts  1.77 us (2%)
    pallas_call x1, Pallas kernels, body(): pl.pallas_call(block_kernel, out_shape=jax.ShapeDtypeStruct(queue.shape,...  86.6 us

profile of v5, /device:TPU:1, one launch (start us, length us, event | category | flops | bytes accessed | tf_op | source)
XLA Modules:
  0.0 88.3 jit_solution(13286784784165555036)
XLA Ops:
  0.0 86.6 %block.1 = bf16[2,32,3072]{2,1,0:T(8,128)(2,1)} custom-call(s32[2]{0:T(128)} %steps_ref.1, f32[3,50,3072]{2,1,0:T(8,128)} %bitcast.4, bf16[2,32,3072]{2,1,0:T(8,128)(2,1)} %queue_hbm.1, bf16[32,3072]{1,0:T(8,128)(2,1)} %noise_hbm.1, f32[2,128]{1,0:T(2,128)} %gains_hbm.1, bf16[8,384,384]{2,1,0:T(8,128)(2,1)} %bitcast.3, bf16[8,16,3072]{2,1,0:T(8,128)(2,1)} %bitcast.5), custom_call_target="tpu_custom_call" | custom-call | tf_op jit(solution)/shard_map/block/pallas_call | solution.py:635
  86.6 1.8 %copy.9 = bf16[2,32,3072]{2,1,0:T(8,128)(2,1)} copy(bf16[2,32,3072]{2,1,0:T(8,128)(2,1)} %block.1) | data formatting | bytes 786432

commit v6 on v5

--- a/solution.py
+++ b/solution.py
@@ -393,7 +393,7 @@
     wq.y_relay(OPP)
     wq.y_end(LEFT)
     copies.got("zrr", "zll")
-    for rel in range(4):
+    for rel in (OPP, LEFT, RIGHT, OWN):
         project_kv(rel, 1)
     share(OPP, 0)
     outs.ring_last()
@@ -401,7 +401,6 @@
     wq.y_end(RIGHT)
     wq.y_end(OPP)
     project_q(OWN)
-    share(OWN, 1)
     wq.done(LEFT)
     dq.got("s1")
     project_q(LEFT)
@@ -409,11 +408,12 @@
     wq.done(RIGHT)
     dq.got("s2")
     project_q(RIGHT)
+    share(OPP, 1)
     share(RIGHT, 1)
+    share(OWN, 1)
     wq.done(OPP)
     dq.got("s3")
     project_q(OPP)
-    share(OPP, 1)
     outs.ring_end()
     names = [f"{rel}{group}" for rel in range(4) for group in range(2)]
 
@@ -474,11 +474,9 @@
     for rel in (LEFT, RIGHT, OPP):
         copies.got(f"aq{rel}", f"bq{rel}")
     first_part(OPP)
-    first_part(RIGHT)
     outs.y_relay(LEFT)
     outs.y_relay(RIGHT)
-    first_part(LEFT)
-    first_part(OWN)
+    first_part(RIGHT)
     outs.y_relay(OPP)
 
     @pl.when(has_beside)
@@ -491,6 +489,7 @@
     attend(RIGHT)
     for rel in (LEFT, RIGHT, OPP):
         outs.y_end(rel)
+    first_part(LEFT)
     attend(LEFT)
     own_wo.wait()
     for rel in (LEFT, RIGHT, OPP):
@@ -503,6 +502,7 @@
         po[2 + j] = p[:, half + j * sub : half + (j + 1) * sub]
         copies.start(f"rl{j}", po.at[j], rl.at[j], me.to(x=1))
         copies.start(f"rr{j}", po.at[2 + j], rr.at[j], me.to(x=-1))
+    first_part(OWN)
     attend(OWN)
 
     right = contribution(RIGHT)

time: 89.6 us -> 88.7 us (0.990); the launches traced: 88.3 us -> 88.5 us
  no operation moved by 1% of the time
where the time goes in v6:
time: 88.7 us; the launch traced here: 88.5 us
  Pallas kernels  86.7 us (98%)
  local copies, waits for them, and re-layouts  1.77 us (2%)
    pallas_call x1, Pallas kernels, body(): pl.pallas_call(block_kernel, out_shape=jax.ShapeDtypeStruct(queue.shape,...  86.7 us

profile of v6, /device:TPU:1, one launch (start us, length us, event | category | flops | bytes accessed | tf_op | source)
XLA Modules:
  0.0 88.5 jit_solution(9947101110321957205)
XLA Ops:
  0.0 86.7 %block.1 = bf16[2,32,3072]{2,1,0:T(8,128)(2,1)} custom-call(s32[2]{0:T(128)} %steps_ref.1, f32[3,50,3072]{2,1,0:T(8,128)} %bitcast.4, bf16[2,32,3072]{2,1,0:T(8,128)(2,1)} %queue_hbm.1, bf16[32,3072]{1,0:T(8,128)(2,1)} %noise_hbm.1, f32[2,128]{1,0:T(2,128)} %gains_hbm.1, bf16[8,384,384]{2,1,0:T(8,128)(2,1)} %bitcast.3, bf16[8,16,3072]{2,1,0:T(8,128)(2,1)} %bitcast.5), custom_call_target="tpu_custom_call" | custom-call | tf_op jit(solution)/shard_map/block/pallas_call | solution.py:635
  86.7 1.8 %copy.9 = bf16[2,32,3072]{2,1,0:T(8,128)(2,1)} copy(bf16[2,32,3072]{2,1,0:T(8,128)(2,1)} %block.1) | data formatting | bytes 786432

commit v7 on v6

--- a/solution.py
+++ b/solution.py
@@ -11,6 +11,7 @@
 NX = 4
 NY = 4
 NZ = 4
+PIECES = 4
 OWN, LEFT, RIGHT, OPP = 0, 1, 2, 3
 
 
@@ -227,7 +228,8 @@
     back = {LEFT: RIGHT, RIGHT: LEFT, OPP: OPP}
     shift = {LEFT: -1, RIGHT: 1, OPP: 2}
 
-    mod_copy = pltpu.make_async_copy(mod_hbm, mod, local.at[6])
+    norm_part, gate_part = pl.ds(0, 2), pl.ds(2, 1)
+    mod_copy = pltpu.make_async_copy(mod_hbm.at[norm_part], mod.at[norm_part], local.at[6])
     mod_copy.start()
     queue_copy = pltpu.make_async_copy(queue_hbm, queue_ref, local.at[7])
     queue_copy.start()
@@ -284,6 +286,8 @@
     wk, dk = gather("k", kv_cols, rows_in * 5 // 12)
     wq, dq = gather("q", q_cols, rows_in // 2)
     wk.ring_start()
+    gate_copy = pltpu.make_async_copy(mod_hbm.at[gate_part], mod.at[gate_part], local.at[22])
+    gate_copy.start()
     own_w = pltpu.make_async_copy(w_hbm, wg.at[OWN], local.at[0])
     own_w.start()
     own_wo = pltpu.make_async_copy(wo_hbm, wo.at[OWN], local.at[1])
@@ -495,37 +499,39 @@
     for rel in (LEFT, RIGHT, OPP):
         outs.done(rel)
 
-    sub = half // 2
+    pieces = PIECES
+    sub = half // pieces
     p = contribution(OPP).astype(bf16)
-    for j in range(2):
+    for j in range(pieces):
         po[j] = p[:, j * sub : (j + 1) * sub]
-        po[2 + j] = p[:, half + j * sub : half + (j + 1) * sub]
+        po[pieces + j] = p[:, half + j * sub : half + (j + 1) * sub]
         copies.start(f"rl{j}", po.at[j], rl.at[j], me.to(x=1))
-        copies.start(f"rr{j}", po.at[2 + j], rr.at[j], me.to(x=-1))
+        copies.start(f"rr{j}", po.at[pieces + j], rr.at[j], me.to(x=-1))
     first_part(OWN)
     attend(OWN)
 
     right = contribution(RIGHT)
-    for j in range(2):
-        pr_s[2 + j] = right[:, half + j * sub : half + (j + 1) * sub].astype(bf16)
-        copies.start(f"fl{2 + j}", pr_s.at[2 + j], fl.at[2 + j], me.to(x=1))
+    for j in range(pieces):
+        pr_s[pieces + j] = right[:, half + j * sub : half + (j + 1) * sub].astype(bf16)
+        copies.start(f"fl{pieces + j}", pr_s.at[pieces + j], fl.at[pieces + j], me.to(x=1))
     left = contribution(LEFT)
-    for j in range(2):
+    for j in range(pieces):
         pl_s[j] = left[:, j * sub : (j + 1) * sub].astype(bf16)
         copies.start(f"fr{j}", pl_s.at[j], fr.at[j], me.to(x=-1))
-    for j in range(2):
+    for j in range(pieces):
         copies.got(f"rl{j}")
         pr_s[j] = (right[:, j * sub : (j + 1) * sub] + rl[j].astype(f32)).astype(bf16)
         copies.start(f"fl{j}", pr_s.at[j], fl.at[j], me.to(x=1))
         copies.got(f"rr{j}")
-        pl_s[2 + j] = (
+        pl_s[pieces + j] = (
             left[:, half + j * sub : half + (j + 1) * sub] + rr[j].astype(f32)
         ).astype(bf16)
-        copies.start(f"fr{2 + j}", pl_s.at[2 + j], fr.at[2 + j], me.to(x=-1))
+        copies.start(f"fr{pieces + j}", pl_s.at[pieces + j], fr.at[pieces + j], me.to(x=-1))
 
     p = contribution(OWN)
     copies.got("qs")
     qb[core] = queue_ref[core]
+    gate_copy.wait()
     gate = mod[2, pl.ds(steps_ref[core], 1), :]
     sends_on = jnp.logical_and(core == 1, frame < frames - 1)
     near, next0, next1, kept = {}, {}, {}, {}
@@ -535,9 +541,9 @@
     def _():
         noise_copy.start()
 
-    for j in range(2):
-        copies.got(f"fl{j}", f"fr{j}", f"fl{2 + j}", f"fr{2 + j}")
-        for h in (j, 2 + j):
+    for j in range(pieces):
+        copies.got(f"fl{j}", f"fr{j}", f"fl{pieces + j}", f"fr{pieces + j}")
+        for h in (j, pieces + j):
             cols = slice(h * sub, (h + 1) * sub)
             proj = p[:, cols] + fl[h].astype(f32) + fr[h].astype(f32)
             for tok in range(2):
@@ -545,61 +551,61 @@
                     qb[tok, :, cols].astype(f32)
                     + gate[:, cols] * proj[tok * rows : (tok + 1) * rows]
                 ).astype(bf16)
-        for h in (j, 2 + j):
+        for h in (j, pieces + j):
             cols = pl.ds(h * sub, sub)
-            kept[h] = pltpu.make_async_copy(ob.at[h, 0], out_hbm.at[1, :, cols], local.at[10 + h])
+            kept[h] = pltpu.make_async_copy(ob.at[h, 0], out_hbm.at[1, :, cols], local.at[32 + h])
             near[h] = copies.make(f"o{h}", ob.at[h, 1], ou.at[1, h], me.to(flip=True))
             next0[h] = copies.make(f"n{h}", ob.at[h, 0], ou.at[0, h], (after, me.head, 0))
             next1[h] = pltpu.make_async_remote_copy(
                 src_ref=ob.at[h, 1], dst_ref=ou.at[0, h],
-                send_sem=local.at[2 + h], recv_sem=recv.at[copies.count - 1],
+                send_sem=local.at[24 + h], recv_sem=recv.at[copies.count - 1],
                 device_id=(after, me.head, 1), device_id_type=MESH,
             )
 
         @pl.when(core == 0)
         def _():
-            for h in (j, 2 + j):
+            for h in (j, pieces + j):
                 near[h].start()
                 kept[h].start()
 
         @pl.when(sends_on)
         def _():
-            for h in (j, 2 + j):
+            for h in (j, pieces + j):
                 next0[h].start()
                 next1[h].start()
 
     def keep(slot, h):
         cols = pl.ds(h * sub, sub)
         return pltpu.make_async_copy(
-            ou.at[slot, h], out_hbm.at[slot, :, cols], local.at[14 + 4 * slot + h]
+            ou.at[slot, h], out_hbm.at[slot, :, cols], local.at[40 + 2 * pieces * slot + h]
         )
 
     @pl.when(core == 1)
     def _():
-        for h in range(4):
+        for h in range(2 * pieces):
             near[h].wait_recv()
             keep(1, h).start()
 
     @pl.when(frame > 0)
     def _():
-        for h in range(4):
+        for h in range(2 * pieces):
             next0[h].wait_recv()
             keep(0, h).start()
 
     @pl.when(core == 0)
     def _():
-        for h in range(4):
+        for h in range(2 * pieces):
             near[h].wait_send()
             kept[h].wait()
 
     @pl.when(core == 1)
     def _():
-        for h in range(4):
+        for h in range(2 * pieces):
             keep(1, h).wait()
 
     @pl.when(frame > 0)
     def _():
-        for h in range(4):
+        for h in range(2 * pieces):
             keep(0, h).wait()
 
     @pl.when(frame == 0)
@@ -608,7 +614,7 @@
 
     @pl.when(sends_on)
     def _():
-        for h in range(4):
+        for h in range(2 * pieces):
             next0[h].wait_send()
             next1[h].wait_send()
 
@@ -617,7 +623,7 @@
         for n in names:
             copies.all["kv" + n].wait_send()
 
-    copies.sent(skip=[f"{t}{h}" for t in "on" for h in range(4)] + ["kv" + n for n in names])
+    copies.sent(skip=[f"{t}{h}" for t in "on" for h in range(2 * pieces)] + ["kv" + n for n in names])
 
 
 def body(queue, timesteps, mod_table, w_qkv, norm_gains, w_out, noise_frame):
@@ -630,7 +636,7 @@
     keys = NX * 2 * tokens
     eighth = width // 8
     half = width // 2
-    sub = half // 2
+    sub = half // PIECES
     table = jnp.transpose(mod_table, (1, 0, 2))
     return pl.pallas_call(
         block_kernel,
@@ -655,19 +661,19 @@
             pltpu.VMEM((NX, NZ, 2 * rows, hs), bf16),
             pltpu.VMEM((NX, NZ, 2 * rows, hs), bf16),
             pltpu.VMEM((NZ, 8, hs // 8, width), bf16),
-            pltpu.VMEM((4, 2 * rows, sub), bf16),
-            pltpu.VMEM((4, 2 * rows, sub), bf16),
-            pltpu.VMEM((4, 2 * rows, sub), bf16),
-            pltpu.VMEM((2, 2 * rows, sub), bf16),
-            pltpu.VMEM((2, 2 * rows, sub), bf16),
-            pltpu.VMEM((4, 2 * rows, sub), bf16),
-            pltpu.VMEM((4, 2 * rows, sub), bf16),
+            pltpu.VMEM((2 * PIECES, 2 * rows, sub), bf16),
+            pltpu.VMEM((2 * PIECES, 2 * rows, sub), bf16),
+            pltpu.VMEM((2 * PIECES, 2 * rows, sub), bf16),
+            pltpu.VMEM((PIECES, 2 * rows, sub), bf16),
+            pltpu.VMEM((PIECES, 2 * rows, sub), bf16),
+            pltpu.VMEM((2 * PIECES, 2 * rows, sub), bf16),
+            pltpu.VMEM((2 * PIECES, 2 * rows, sub), bf16),
             pltpu.VMEM((2, rows, width), bf16),
-            pltpu.VMEM((4, 2, rows, sub), bf16),
-            pltpu.VMEM((2, 4, rows, sub), bf16),
-            pltpu.SemaphoreType.DMA((22,)),
-            pltpu.SemaphoreType.DMA((200,)),
-            pltpu.SemaphoreType.DMA((200,)),
+            pltpu.VMEM((2 * PIECES, 2, rows, sub), bf16),
+            pltpu.VMEM((2, 2 * PIECES, rows, sub), bf16),
+            pltpu.SemaphoreType.DMA((56,)),
+            pltpu.SemaphoreType.DMA((224,)),
+            pltpu.SemaphoreType.DMA((224,)),
         ],
         compiler_params=pltpu.CompilerParams(
             collective_id=0, has_side_effects=True, vmem_limit_bytes=56 * 1024 * 1024

time: 88.7 us -> 88.6 us (level)
  no operation moved by 1% of the time
where the time goes in v7:
time: 88.6 us; the launch traced here: 88.5 us
  Pallas kernels  86.7 us (98%)
  local copies, waits for them, and re-layouts  1.77 us (2%)
    pallas_call x1, Pallas kernels, body(): pl.pallas_call(block_kernel, out_shape=jax.ShapeDtypeStruct(queue.shape,...  86.7 us

profile of v7, /device:TPU:1, one launch (start us, length us, event | category | flops | bytes accessed | tf_op | source)
XLA Modules:
  0.0 88.5 jit_solution(4204180773198923647)
XLA Ops:
  0.0 86.7 %block.1 = bf16[2,32,3072]{2,1,0:T(8,128)(2,1)} custom-call(s32[2]{0:T(128)} %steps_ref.1, f32[3,50,3072]{2,1,0:T(8,128)} %bitcast.4, bf16[2,32,3072]{2,1,0:T(8,128)(2,1)} %queue_hbm.1, bf16[32,3072]{1,0:T(8,128)(2,1)} %noise_hbm.1, f32[2,128]{1,0:T(2,128)} %gains_hbm.1, bf16[8,384,384]{2,1,0:T(8,128)(2,1)} %bitcast.3, bf16[8,16,3072]{2,1,0:T(8,128)(2,1)} %bitcast.5), custom_call_target="tpu_custom_call" | custom-call | tf_op jit(solution)/shard_map/block/pallas_call | solution.py:641
  86.7 1.8 %copy.9 = bf16[2,32,3072]{2,1,0:T(8,128)(2,1)} copy(bf16[2,32,3072]{2,1,0:T(8,128)(2,1)} %block.1) | data formatting | bytes 786432
